TPU v7x, 128 devices: a whole 4x4x4 slice. The times are simulated.
128 devices in a mesh: gx: 16 (over x, z), gy: 8 (over y, core).
Axes of the slice: x: 4, y: 4, z: 4, core: 2. Of those that a mesh axis runs over, the one named last changes fastest.
Arguments:
- swath_bands: bfloat16 [131072, 6, 128], P(('gx', 'gy')), may hold values from 0 to 1
- clear_weight: bfloat16 [131072, 128], P(('gx', 'gy')), may hold values from 0.049804688 to 1
- owners: int32 [131072, 1], P(('gx', 'gy')), may hold values from 0 to 127; in each aligned block of 1024 rows (0 to 1023, 1024 to 2047, ...) at most 12 rows name the same one
- tile_row: int32 [131072], P(('gx', 'gy')), may hold values from 0 to 255
- columns: int32 [131072, 128], P(('gx', 'gy')), may hold values from 0 to 255
- counts: int32 [128], P(('gx', 'gy')), may hold values from 1 to 1024, 98304 in all
- conduct_x: float32 [2048, 4096], P('gy', 'gx'), may hold values from 0.02 to 0.2
- conduct_y: float32 [2048, 4096], P('gy', 'gx'), may hold values from 0.02 to 0.2
Outputs:
- gridded: float32 [6, 2048, 4096], P(None, 'gy', 'gx')
- coverage: float32 [2048, 4096], P('gy', 'gx')
Inputs may be any that keep to these rules, and one draw needn't show every extreme that they name: `owners`: within the rows of one device no owner is named by more than 12 blocks, a bound that some block reaches. The counts sum to 98304, and some device's count is 1024.
All inputs are finite; a program needn't handle non-finite values.
Results may differ from a plain program's by a relative error of at most 0.0017.
Values may be sent and summed in bfloat16 or wider, within the bound.
No kernel may reach another device: no remote copies, remote signals or barrier semaphores. Data moves between devices by JAX's collectives and lax.ppermute only.
A program may use at most 64 MiB of HBM per device.

v0:
```python
import functools

import jax
import jax.numpy as jnp
from jax import lax
from jax.experimental import pallas as pl
from jax.experimental.pallas import tpu as pltpu
from jax.sharding import PartitionSpec as P

CAPACITY = 12
SLOTS = CAPACITY + 1
COUNT_LANE = 14
CODES = 16
ENTRIES = 896
GROUP = 64
ROWS = 16
FLOOR = 0.15
HALO = 2

f32 = jnp.float32
bf16 = jnp.bfloat16
i32 = jnp.int32


def iota(shape, dim):
    return lax.broadcasted_iota(i32, shape, dim)


def ring(count, step):
    return [(i, (i + step) % count) for i in range(count)]


def pack_kernel(
    count_ref,
    owner_ref,
    row_ref,
    swath_ref,
    weight_ref,
    cols_ref,
    out_ref,
    done_ref,
    owner_v,
    row_v,
    swath_v,
    weight_v,
    cols_v,
    rows_f,
    codes_f,
    slot_v,
    slot_s,
    sem,
    load_sems,
):
    bands, blocks, _ = swath_ref.shape
    loads = [
        pltpu.make_async_copy(source, target, load_sems.at[i])
        for i, (source, target) in enumerate(
            (
                (owner_ref, owner_v),
                (row_ref, row_v),
                (weight_ref, weight_v),
                (cols_ref, cols_v),
                (swath_ref, swath_v),
            )
        )
    ]
    for load in loads:
        load.start()
    done_ref[...] = jnp.zeros((8, 128), f32)
    devices = out_ref.shape[0] // SLOTS
    live_count = count_ref[0]
    earlier = (iota((blocks, blocks), 0) < iota((blocks, blocks), 1)).astype(f32).astype(bf16)

    @pl.loop(0, devices // 2)
    def _(t):
        out_ref[pl.ds(t * 2 * SLOTS, 2 * SLOTS)] = jnp.zeros((2 * SLOTS, 8, 128), bf16)

    loads[0].wait()
    owner = owner_v[...]
    live = iota((1, blocks), 1) < live_count
    owner = jnp.where(live, owner, -1)
    named = (iota((devices, blocks), 0) == owner).astype(f32)
    named16 = named.astype(bf16)
    before = jnp.dot(named16, earlier, preferred_element_type=f32)
    rank = jnp.sum(named * before, axis=0, keepdims=True).astype(i32)
    slot_v[...] = jnp.where(live, owner * SLOTS + rank, CAPACITY)
    copy = pltpu.make_async_copy(slot_v, slot_s, sem)
    copy.start()
    entry = iota((128, blocks), 0)
    loads[1].wait()
    place = jnp.where(entry == rank, (row_v[...] + 1).astype(f32), 0.0)
    place = jnp.where(entry == COUNT_LANE, 1.0, place).astype(bf16)
    codes_f[...] = lax.dot_general(
        named16, place, (((1,), (1,)), ((), ())), preferred_element_type=f32
    )

    for load in loads[2:]:
        load.wait()

    @pl.loop(0, blocks // 16, unroll=4)
    def _(g):
        near = pl.ds(pl.multiple_of(g * 16, 16), 16)
        weight = weight_v[near, :].astype(f32)
        for c in range(bands):
            rows_f[pl.ds(g * 128 + c, 16, stride=8), :] = swath_v[c, near, :].astype(f32) * weight
        rows_f[pl.ds(g * 128 + bands, 16, stride=8), :] = weight
        rows_f[pl.ds(g * 128 + bands + 1, 16, stride=8), :] = cols_v[near, :].astype(f32)

    copy.wait()

    @pl.loop(0, (live_count + 15) // 16)
    def _(group):
        for i in range(16):
            b = group * 16 + i
            out_ref[slot_s[0, b]] = rows_f[pl.ds(pl.multiple_of(b * 8, 8), 8), :].astype(bf16)

    @pl.loop(0, devices, unroll=4)
    def _(t):
        code = codes_f[pl.ds(t, 1), :]
        out_ref[t * SLOTS + CAPACITY] = jnp.broadcast_to(code, (8, 128)).astype(bf16)


def pack(counts, owners, tile_row, swath, weight, columns, devices):
    blocks = weight.shape[0]
    vmem = pl.BlockSpec(memory_space=pltpu.VMEM)
    return pl.pallas_call(
        pack_kernel,
        out_shape=(
            jax.ShapeDtypeStruct((devices * SLOTS, 8, 128), bf16),
            jax.ShapeDtypeStruct((8, 128), f32),
        ),
        in_specs=[pl.BlockSpec(memory_space=pltpu.SMEM)]
        + [pl.BlockSpec(memory_space=pltpu.HBM)] * 5,
        out_specs=(vmem, vmem),
        scratch_shapes=[
            pltpu.VMEM((1, blocks), i32),
            pltpu.VMEM((1, blocks), i32),
            pltpu.VMEM(swath.shape, bf16),
            pltpu.VMEM(weight.shape, bf16),
            pltpu.VMEM(columns.shape, i32),
            pltpu.VMEM((blocks * 8, 128), f32),
            pltpu.VMEM((devices, 128), f32),
            pltpu.VMEM((1, blocks), i32),
            pltpu.SMEM((1, blocks), i32),
            pltpu.SemaphoreType.DMA,
            pltpu.SemaphoreType.DMA((5,)),
        ],
        compiler_params=pltpu.CompilerParams(vmem_limit_bytes=60 << 20),
        name="pack",
    )(counts, owners, tile_row, swath, weight, columns)


def bin_kernel(
    msg_ref,
    edge_top,
    edge_bottom,
    acc_ref,
    top_ref,
    bottom_ref,
    codes_v,
    lists_v,
    lists_s,
    sem,
):
    sources = msg_ref.shape[0] // SLOTS
    height = acc_ref.shape[0] - 1

    @pl.loop(0, sources // 8)
    def _(g):
        for i in range(8):
            s = g * 8 + i
            tile = msg_ref[s * SLOTS + CAPACITY].astype(f32)
            codes_v[pl.ds(s, 1), :] = tile[0:1, :]

    codes = codes_v[...].T[0:CODES, :]
    pairs = jnp.floor((codes[COUNT_LANE : COUNT_LANE + 1, :] + 1.0) * 0.5)
    earlier = (iota((sources, sources), 0) < iota((sources, sources), 1)).astype(f32).astype(bf16)
    before = jnp.dot(
        jnp.broadcast_to(pairs, (8, sources)).astype(bf16), earlier, preferred_element_type=f32
    )[0:1, :]
    total = (before + pairs)[:, sources - 1 : sources]
    entry = iota((ENTRIES, sources), 0).astype(f32)
    source = iota((1, sources), 1).astype(f32)
    facts, places = [], []
    for p in range(CAPACITY // 2):
        facts.append(
            jnp.concatenate(
                [
                    codes[2 * p : 2 * p + 2, :],
                    source,
                    jnp.full((1, sources), 2.0 * p, f32),
                    jnp.zeros((4, sources), f32),
                ],
                axis=0,
            ).astype(bf16)
        )
        place = jnp.where(pairs > p, before + p, -1.0)
        places.append(jnp.where(entry == place, 1.0, 0.0).astype(bf16))
    found = lax.dot_general(
        jnp.concatenate(facts, axis=1),
        jnp.concatenate(places, axis=1),
        (((1,), (1,)), ((), ())),
        preferred_element_type=f32,
    )
    rows = jnp.where(found[0:2] > 0.0, found[0:2] - 1.0, float(height))
    slots = found[2:3] * SLOTS + found[3:4]
    lists_v[0:1, :] = slots.astype(i32)
    lists_v[1:3, :] = rows.astype(i32)
    lists_v[3:4, :] = jnp.broadcast_to(total, (1, ENTRIES)).astype(i32)
    copy = pltpu.make_async_copy(lists_v, lists_s, sem)
    copy.start()

    @pl.loop(0, height // 16)
    def _(g):
        acc_ref[pl.ds(g * 16, 16)] = jnp.zeros((16, 32, 128), f32)

    acc_ref[height] = jnp.zeros((32, 128), f32)
    copy.wait()
    low_ids = iota((64, 128), 0).astype(f32)
    quarter_ids = (iota((32, 128), 0) // 8).astype(f32)
    empty = jnp.zeros((32, 128), bf16)

    @pl.loop(0, (lists_s[3, 0] + GROUP - 1) // GROUP)
    def _(group):
        for j in range(GROUP):
            slot = lists_s[0, group * GROUP + j]
            values, hits = [], []
            for i in range(2):
                block = msg_ref[slot + i].astype(f32)
                col = block[7:8, :]
                quarter = jnp.where(
                    col >= 128.0,
                    jnp.where(col >= 192.0, 3.0, 2.0),
                    jnp.where(col >= 64.0, 1.0, 0.0),
                )
                low = col - 64.0 * quarter
                block4 = jnp.concatenate([block] * 4, axis=0)
                values.append(jnp.where(quarter_ids == quarter, block4, 0.0).astype(bf16))
                hits.append(jnp.where(low_ids == low, 1.0, 0.0).astype(bf16))
            values = jnp.concatenate(
                [
                    jnp.concatenate([values[0], empty], axis=1),
                    jnp.concatenate([empty, values[1]], axis=1),
                ],
                axis=0,
            )
            sums = lax.dot_general(
                values,
                jnp.concatenate(hits, axis=1),
                (((1,), (1,)), ((), ())),
                preferred_element_type=f32,
            )
            row_0 = lists_s[1, group * GROUP + j]
            row_1 = lists_s[2, group * GROUP + j]
            shared = jnp.where(row_0 == row_1, sums[0:32], 0.0)
            sum_0 = acc_ref[row_0, :, 0:64] + sums[0:32]
            sum_1 = acc_ref[row_1, :, 0:64] + (sums[32:64] + shared)
            acc_ref[row_0, :, 0:64] = sum_0
            acc_ref[row_1, :, 0:64] = sum_1

    for ref, first, edge in ((top_ref, 0, edge_top), (bottom_ref, height - HALO, edge_bottom)):
        for i in range(HALO):
            for h, half in enumerate(join_quarters(acc_ref[first + i])):
                ref[i, :, 128 * h : 128 * h + 128] = half
        ref[HALO] = edge[...]


def join_quarters(tile):
    quarters = [tile[8 * q : 8 * q + 8] for q in range(4)]
    return [quarters[2 * h] + pltpu.roll(quarters[2 * h + 1], 64, 1) for h in range(2)]


def bin_blocks(message, edge_top, edge_bottom, height, width):
    sources = message.shape[0] // SLOTS
    vmem = pl.BlockSpec(memory_space=pltpu.VMEM)
    shape = lambda *dims: jax.ShapeDtypeStruct(dims, f32)
    return pl.pallas_call(
        bin_kernel,
        out_shape=(
            shape(height + 1, 32, 128),
            shape(HALO + 1, 8, width),
            shape(HALO + 1, 8, width),
        ),
        in_specs=[vmem] * 3,
        out_specs=(vmem,) * 3,
        scratch_shapes=[
            pltpu.VMEM((sources, 128), f32),
            pltpu.VMEM((8, ENTRIES), i32),
            pltpu.SMEM((8, ENTRIES), i32),
            pltpu.SemaphoreType.DMA,
        ],
        compiler_params=pltpu.CompilerParams(vmem_limit_bytes=16 << 20),
        name="bin",
    )(message, edge_top, edge_bottom)


def join_kernel(acc_ref, edge_left, edge_right, fields_ref, left_ref, right_ref):
    lane = iota((8, 128), 1)
    blank = jnp.zeros((8, 128), f32)

    def join_rows(j, carry):
        here = lane // 2 == j
        result = []
        for q in range(4):
            row = q * 64 + j
            first, last = join_quarters(acc_ref[row])
            fields_ref[row, :, 0:128] = first
            fields_ref[row, :, 128:256] = last
            result.append(jnp.where(here, pltpu.roll(first, 2 * j, 1), carry[2 * q]))
            result.append(jnp.where(here, pltpu.roll(last, 2 * j + 2, 1), carry[2 * q + 1]))
        return tuple(result)

    strips = lax.fori_loop(0, 64, join_rows, (blank,) * 8, unroll=8)
    for q in range(4):
        left_ref[q] = strips[2 * q]
        right_ref[q] = strips[2 * q + 1]
    left_ref[4] = edge_left[...]
    right_ref[4] = edge_right[...]


def join(acc, edge_left, edge_right, height, width):
    vmem = pl.BlockSpec(memory_space=pltpu.VMEM)
    shape = lambda *dims: jax.ShapeDtypeStruct(dims, f32)
    return pl.pallas_call(
        join_kernel,
        out_shape=(
            shape(height, 8, width),
            shape(height // 64 + 1, 8, 128),
            shape(height // 64 + 1, 8, 128),
        ),
        in_specs=[vmem] * 3,
        out_specs=(vmem,) * 3,
        compiler_params=pltpu.CompilerParams(vmem_limit_bytes=12 << 20),
        name="join",
    )(acc, edge_left, edge_right)


def relax(current, east_west, north_south, along_x, along_y):
    return current + along_x * (east_west - 2.0 * current) + along_y * (north_south - 2.0 * current)


def smooth_row(above, current, below, near, along_x, along_y):
    lane = iota((8, 128), 1)
    ahead = [pltpu.roll(half, 1, 1) for half in current]
    back = [pltpu.roll(half, 127, 1) for half in current]
    west = [jnp.where(lane == 0, near, ahead[0]), jnp.where(lane == 0, ahead[0], ahead[1])]
    east = [jnp.where(lane == 127, back[1], back[0]), jnp.where(lane == 127, near, back[1])]
    return [
        relax(current[h], east[h] + west[h], below[h] + above[h], along_x[h], along_y[h])
        for h in range(2)
    ]


def smooth_kernel(
    flags_ref,
    acc_ref,
    up_ref,
    down_ref,
    west_ref,
    east_ref,
    cx_ref,
    cy_ref,
    gridded_ref,
    coverage_ref,
    mix_near,
    mix_far,
    near,
    far,
    once,
    once_near,
    twice,
    side_x,
    side_y,
):
    height, _, width = acc_ref.shape
    has_up, has_down = flags_ref[0] > 0, flags_ref[1] > 0
    has_west, has_east = flags_ref[2] > 0, flags_ref[3] > 0
    lane = iota((8, 128), 1)

    def halves(ref, row):
        return [ref[row, :, 0:128], ref[row, :, 128:256]]

    def keep(flag, parts):
        return [jnp.where(flag, part, 0.0) for part in parts]

    def along(ref, row):
        line = ref[pl.ds(row, 1), :]
        return [line[:, i : i + 128] for i in (0, 128)]

    for q in range(4):
        west = jnp.where(has_west, west_ref[q], 0.0)
        east = jnp.where(has_east, east_ref[q], 0.0)
        even = lane % 2 == 0
        mix_near[q] = jnp.where(even, pltpu.roll(west, 127, 1), pltpu.roll(east, 127, 1))
        mix_far[q] = jnp.where(even, west, pltpu.roll(east, 126, 1))

    @pl.loop(0, 64, unroll=16)
    def _(j):
        for q in range(4):
            near[q * 64 + j + 1] = pltpu.roll(mix_near[q], 128 - 2 * j, 1)
            far[q * 64 + j] = pltpu.roll(mix_far[q], 128 - 2 * j, 1)

    for tile, row, flag in ((5, 0, has_up), (6, height + 1, has_down)):
        west = jnp.where(has_west & flag, west_ref[tile], 0.0)
        east = jnp.where(has_east & flag, east_ref[tile], 0.0)
        near[row] = jnp.where(lane < 64, pltpu.roll(west, 1, 1), pltpu.roll(east, 127, 1))

    upper = iota((128, 128), 0) < 64
    for i, side in enumerate((side_x, side_y)):
        for half in range(2):
            at = slice(2 * i + half, 2 * i + half + 1)
            west = jnp.where(has_west, west_ref[4, at, :], 0.0)
            east = jnp.where(has_east, east_ref[4, at, :], 0.0)
            both = jnp.where(
                upper, jnp.broadcast_to(west, (128, 128)), jnp.broadcast_to(east, (128, 128))
            )
            side[half * 128 : half * 128 + 128, :] = both.T

    up = [keep(has_up, halves(up_ref, i)) for i in range(2)]
    down = [keep(has_down, halves(down_ref, i)) for i in range(2)]

    def store(ref, row, parts):
        ref[row, :, 0:128] = parts[0]
        ref[row, :, 128:256] = parts[1]

    def coefficients(row):
        return along(cx_ref, row), along(cy_ref, row)

    def beyond(ref, flag):
        return [
            keep(flag, [ref[HALO, i : i + 1, h * 128 : h * 128 + 128] for h in range(2)])
            for i in range(2)
        ]

    store(
        once,
        0,
        smooth_row(up[0], up[1], halves(acc_ref, 0), near[0], *beyond(up_ref, has_up)),
    )
    store(
        once,
        height + 1,
        smooth_row(
            halves(acc_ref, height - 1),
            down[0],
            down[1],
            near[height + 1],
            *beyond(down_ref, has_down),
        ),
    )
    steps = height // ROWS

    @pl.loop(0, steps + 3)
    def _(g):
        block = jnp.clip(g - 3, 0, steps - 1)
        for part in range(ROWS // 8):
            base = block * ROWS + part * 8
            rows = pl.ds(pl.multiple_of(base, 8), 8)
            for half in range(width // 128):
                cols = pl.ds(half * 128, 128)
                coverage = twice[half, pl.ds(base * 8 + 6, 8, stride=8), :]
                coverage_ref[rows, cols] = coverage
                scale = 1.0 / jnp.maximum(coverage, FLOOR)
                for c in range(6):
                    gridded_ref[c, rows, cols] = (
                        twice[half, pl.ds(base * 8 + c, 8, stride=8), :] * scale
                    )
        start = jnp.clip(g - 2, 0, steps - 1) * ROWS
        lines = [halves(once, start + i) for i in range(ROWS + 2)]
        for i in range(ROWS):
            fresh = smooth_row(
                *lines[i : i + 3], once_near[start + i], *coefficients(start + i)
            )
            for half in range(2):
                twice[half, pl.ds(pl.multiple_of((start + i) * 8, 8), 8), :] = fresh[half]
        block = jnp.minimum(g, steps - 1)
        start = block * ROWS
        lines = [halves(acc_ref, start + i) for i in range(ROWS)]
        before = halves(acc_ref, jnp.maximum(start - 1, 0))
        after = halves(acc_ref, jnp.minimum(start + ROWS, height - 1))
        before = [jnp.where(block == 0, up[1][h], before[h]) for h in range(2)]
        after = [jnp.where(block == steps - 1, down[0][h], after[h]) for h in range(2)]
        lines = [before] + lines + [after]
        for i in range(ROWS):
            row = start + i + 1
            along_x, along_y = coefficients(start + i)
            store(once, row, smooth_row(*lines[i : i + 3], near[row], along_x, along_y))
            inner = jnp.where(lane < 64, lines[i + 1][0], lines[i + 1][1])
            once_near[start + i] = relax(
                near[row],
                inner + far[start + i],
                near[row + 1] + near[row - 1],
                side_x[pl.ds(start + i, 1), :],
                side_y[pl.ds(start + i, 1), :],
            )


def smooth(flags, acc, up, down, west, east, cx, cy):
    height, _, width = acc.shape
    vmem = pl.BlockSpec(memory_space=pltpu.VMEM)
    return pl.pallas_call(
        smooth_kernel,
        out_shape=(
            jax.ShapeDtypeStruct((6, height, width), f32),
            jax.ShapeDtypeStruct((height, width), f32),
        ),
        in_specs=[pl.BlockSpec(memory_space=pltpu.SMEM)] + [vmem] * 7,
        out_specs=(vmem, vmem),
        scratch_shapes=[
            pltpu.VMEM((4, 8, 128), f32),
            pltpu.VMEM((4, 8, 128), f32),
            pltpu.VMEM((height + 2, 8, 128), f32),
            pltpu.VMEM((height, 8, 128), f32),
            pltpu.VMEM((height + 2, 8, width), f32),
            pltpu.VMEM((height, 8, 128), f32),
            pltpu.VMEM((width // 128, height * 8, 128), f32),
            pltpu.VMEM((height, 128), f32),
            pltpu.VMEM((height, 128), f32),
        ],
        compiler_params=pltpu.CompilerParams(vmem_limit_bytes=24 << 20),
        name="smooth",
    )(flags, acc, up, down, west, east, cx, cy)


def edge_kernel(after_ref, flags_ref, cx_ref, cy_ref, top_ref, bottom_ref, left_ref, right_ref):
    height, width = cx_ref.shape
    for ref in (top_ref, bottom_ref, left_ref, right_ref):
        ref[...] = jnp.zeros_like(ref)
    for i, block in enumerate((cx_ref, cy_ref)):
        top_ref[i : i + 1, :] = block[0:1, :]
        bottom_ref[i : i + 1, :] = block[height - 1 : height, :]
        first = block[:, 0:128].T
        last = block[:, width - 128 : width].T
        for half in range(2):
            at = slice(2 * i + half, 2 * i + half + 1)
            left_ref[at, :] = first[0:1, half * 128 : half * 128 + 128]
            right_ref[at, :] = last[127:128, half * 128 : half * 128 + 128]


def coefficient_edges(after, flags, cx, cy):
    width = cx.shape[1]
    vmem = pl.BlockSpec(memory_space=pltpu.VMEM)
    row = jax.ShapeDtypeStruct((8, width), f32)
    column = jax.ShapeDtypeStruct((8, 128), f32)
    return pl.pallas_call(
        edge_kernel,
        out_shape=(row, row, column, column),
        in_specs=[vmem, pl.BlockSpec(memory_space=pltpu.SMEM), vmem, vmem],
        out_specs=(vmem,) * 4,
        compiler_params=pltpu.CompilerParams(vmem_limit_bytes=8 << 20),
        name="coefficient_edges",
    )(after, flags, cx, cy)


def body(swath_bands, clear_weight, owners, tile_row, columns, counts, conduct_x, conduct_y):
    blocks = swath_bands.shape[0]
    height, width = conduct_x.shape
    across, along = lax.axis_size("gx"), lax.axis_size("gy")
    devices = across * along
    gx, gy = lax.axis_index("gx"), lax.axis_index("gy")
    flags = jnp.stack([gy > 0, gy < along - 1, gx > 0, gx < across - 1]).astype(i32)
    message, packed = pack(
        counts,
        owners.reshape(1, blocks),
        tile_row.reshape(1, blocks),
        jnp.transpose(swath_bands, (1, 0, 2)),
        clear_weight,
        columns,
        devices,
    )
    arrived = lax.all_to_all(
        message.reshape(devices, SLOTS, 8, 128),
        ("gx", "gy"),
        split_axis=0,
        concat_axis=0,
        tiled=True,
    ).reshape(devices * SLOTS, 8, 128)

    edges = coefficient_edges(packed, flags, conduct_x, conduct_y)
    acc, top, bottom = bin_blocks(arrived, edges[0], edges[1], height, width)
    fields, left, right = join(acc, edges[2], edges[3], height, width)
    up = lax.ppermute(bottom, "gy", ring(along, 1))
    down = lax.ppermute(top, "gy", ring(along, -1))
    near = jnp.concatenate([left, up[1:2, :, 0:128], down[0:1, :, 0:128]], axis=0)
    far = jnp.concatenate([right, up[1:2, :, width - 128 :], down[0:1, :, width - 128 :]], axis=0)
    west = lax.ppermute(far, "gx", ring(across, 1))
    east = lax.ppermute(near, "gx", ring(across, -1))
    return smooth(flags, fields, up, down, west, east, conduct_x, conduct_y)


def solution(mesh):
    return jax.shard_map(
        body,
        mesh=mesh,
        in_specs=(
            P(("gx", "gy"), None, None),
            P(("gx", "gy"), None),
            P(("gx", "gy"), None),
            P(("gx", "gy")),
            P(("gx", "gy"), None),
            P(("gx", "gy")),
            P("gy", "gx"),
            P("gy", "gx"),
        ),
        out_specs=(P(None, "gy", "gx"), P("gy", "gx")),
        check_vma=False,
    )
```

profile of v0, /device:TPU:0, one launch (start us, length us, event | category | flops | bytes accessed | tf_op | source)
XLA Modules:
  0.0 89.8 jit_solution(17389967030862584025)
XLA Ops:
  1.3 5.4 %pack.1 = (bf16[1664,8,128]{2,1,0:T(8,128)(2,1)}, f32[8,128]{1,0:T(8,128)}) custom-call(s32[1]{0:T(128)S(6)} %copy.10.count_ref, s32[1,1024]{1,0:T(1,128)} %bitcast.12, s32[1,1024]{1,0:T(1,128)} %bitcast.13, bf16[6,1024,128]{2,1,0:T(8,128)(2,1)} %bitcast.11, bf16[1024,128]{1,0:T(8,128)(2,1)} %weight_ref.1, s32[1024,128]{1,0:T(8,128)} %cols_ref.1), custom_call_target="tpu_custom_call" | custom-call | tf_op jit(solution)/shard_map/pack/pallas_call | solution.py:126
  6.7 0.0 copy-start.4
  6.7 11.3 %all-to-all-start = ((bf16[128,13,8,128]{3,2,1,0:T(8,128)(2,1)}), bf16[128,13,8,128]{3,2,1,0:T(8,128)(2,1)S(1)}, u32[]{:S(2)}, u32[]{:S(2)}) async-start(bf16[128,13,8,128]{3,2,1,0:T(8,128)(2,1)} %bitcast.10), calls=%async_computation | async-start | bytes 6815744 | tf_op jit(solution)/shard_map/all_to_all | solution.py:571
  18.1 0.1 add_convert_fusion.flags_ref
  18.1 0.0 copy-done.4
  18.1 0.0 copy-start
  18.2 1.0 %copy-done = f32[256,256]{1,0:T(8,128)S(1)} copy-done((f32[256,256]{1,0:T(8,128)S(1)}, f32[256,256]{1,0:T(8,128)}, u32[]{:S(2)}) %copy-start) | copy-done | bytes 262168
  19.1 0.0 copy-start.2
  19.1 0.9 %copy-done.2 = f32[256,256]{1,0:T(8,128)S(1)} copy-done((f32[256,256]{1,0:T(8,128)S(1)}, f32[256,256]{1,0:T(8,128)}, u32[]{:S(2)}) %copy-start.2) | copy-done | bytes 262168
  20.1 0.7 coefficient_edges.1
  20.8 41.8 %all-to-all-done = bf16[128,13,8,128]{3,2,1,0:T(8,128)(2,1)S(1)} async-done(((bf16[128,13,8,128]{3,2,1,0:T(8,128)(2,1)}), bf16[128,13,8,128]{3,2,1,0:T(8,128)(2,1)S(1)}, u32[]{:S(2)}, u32[]{:S(2)}) %all-to-all-start) | async-done | bytes 3407904 | tf_op jit(solution)/shard_map/all_to_all | solution.py:571
  62.6 0.0 copy-start.1
  62.6 0.0 copy-start.3
  62.6 7.7 %bin.1 = (f32[257,32,128]{2,1,0:T(8,128)S(1)}, f32[3,8,256]{2,1,0:T(8,128)S(1)}, f32[3,8,256]{2,1,0:T(8,128)S(1)}) custom-call(bf16[1664,8,128]{2,1,0:T(8,128)(2,1)S(1)} %bitcast.9, f32[8,256]{1,0:T(8,128)S(1)} %get-tuple-element.16.edge_top, f32[8,256]{1,0:T(8,128)S(1)} %get-tuple-element.17.edge_bottom), custom_call_target="tpu_custom_call" | custom-call | tf_op jit(solution)/shard_map/bin/pallas_call | solution.py:277
  70.3 0.0 collective-permute-start
  70.3 2.9 %collective-permute-start.1 = (f32[3,8,256]{2,1,0:T(8,128)S(1)}, f32[3,8,256]{2,1,0:T(8,128)S(1)}, u32[]{:S(2)}, u32[]{:S(2)}) collective-permute-start(f32[3,8,256]{2,1,0:T(8,128)S(1)} %get-tuple-element.23), channel_id=1, source_target_pairs={{0,7},{1,0},{2,1},{3,2},{4,3},{5,4},{6,5},{7,6},{8,15},{9,8},{10,9... | collective-permute-start | bytes 73736 | tf_op jit(solution)/shard_map/ppermute | solution.py:583
  73.2 2.1 %join.1 = (f32[256,8,256]{2,1,0:T(8,128)S(1)}, f32[5,8,128]{2,1,0:T(8,128)S(1)}, f32[5,8,128]{2,1,0:T(8,128)S(1)}) custom-call(f32[257,32,128]{2,1,0:T(8,128)S(1)} %get-tuple-element.18.acc_ref, f32[8,128]{1,0:T(8,128)S(1)} %get-tuple-element.19.edge_left, f32[8,128]{1,0:T(8,128)S(1)} %get-tuple-element.20.edge_right), custom_call_target="tpu_custom_call" | custom-call | tf_op jit(solution)/shard_map/join/pallas_call | solution.py:324
  75.4 0.0 collective-permute-done.up_ref
  75.4 0.0 collective-permute-done.1.down_ref
  75.4 2.4 %collective-permute-start.2 = (f32[7,8,128]{2,1,0:T(8,128)S(1)}, f32[7,8,128]{2,1,0:T(8,128)S(1)}, u32[]{:S(2)}, u32[]{:S(2)}) collective-permute-start(f32[7,8,128]{2,1,0:T(8,128)S(1)} %pad_maximum_fusion), channel_id=1, source_target_pairs={{0,8},{8,16},{16,24},{24,32},{32,40},{40,48},{48,56},{56,64},{64,7... | collective-permute-start | bytes 86024 | tf_op jit(solution)/shard_map/ppermute | solution.py:586
  77.8 3.0 %collective-permute-start.3 = (f32[7,8,128]{2,1,0:T(8,128)S(1)}, f32[7,8,128]{2,1,0:T(8,128)S(1)}, u32[]{:S(2)}, u32[]{:S(2)}) collective-permute-start(f32[7,8,128]{2,1,0:T(8,128)S(1)} %pad_maximum_fusion.1), channel_id=1, source_target_pairs={{0,120},{8,0},{16,8},{24,16},{32,24},{40,32},{48,40},{56,48},{64,5... | collective-permute-start | bytes 86024 | tf_op jit(solution)/shard_map/ppermute | solution.py:587
  80.8 2.0 %collective-permute-done.2.west_ref = f32[7,8,128]{2,1,0:T(8,128)S(1)} collective-permute-done((f32[7,8,128]{2,1,0:T(8,128)S(1)}, f32[7,8,128]{2,1,0:T(8,128)S(1)}, u32[]{:S(2)}, u32[]{:S(2)}) %collective-permute-start.2) | collective-permute-done | bytes 28704 | tf_op jit(solution)/shard_map/ppermute | solution.py:586
  82.8 0.0 collective-permute-done.3.east_ref
  82.8 0.0 copy-done.1
  82.8 0.0 copy-done.3
  82.8 7.0 %smooth.1 = (f32[6,256,256]{2,1,0:T(8,128)}, f32[256,256]{1,0:T(8,128)}) custom-call(s32[4]{0:T(128)S(1)} %add_convert_fusion.flags_ref, f32[256,8,256]{2,1,0:T(8,128)S(1)} %get-tuple-element.21.acc_ref, f32[3,8,256]{2,1,0:T(8,128)S(1)} %collective-permute-done.up_ref, f32[3,8,256]{2,1,0:T(8,128)S(1)} %collective-permute-done.1.down_ref, ...), custom_call_target="tpu_custom_call" | custom-call | tf_op jit(solution)/shard_map/smooth/pallas_call | solution.py:501
  (4 shorter events, 0.0 us)
Async XLA Ops:
  6.7 11.4 %copy-start.4 = (f32[8,128]{1,0:T(8,128)S(1)}, f32[8,128]{1,0:T(8,128)}, u32[]{:S(2)}) copy-start(f32[8,128]{1,0:T(8,128)} %get-tuple-element.15.after_ref) | copy-start | bytes 12292
  6.7 55.9 %all-to-all-start = ((bf16[128,13,8,128]{3,2,1,0:T(8,128)(2,1)}), bf16[128,13,8,128]{3,2,1,0:T(8,128)(2,1)S(1)}, u32[]{:S(2)}, u32[]{:S(2)}) async-start(bf16[128,13,8,128]{3,2,1,0:T(8,128)(2,1)} %bitcast.10), calls=%async_computation | async-start | bytes 6815744 | tf_op jit(solution)/shard_map/all_to_all | solution.py:571
  18.1 1.0 %copy-start = (f32[256,256]{1,0:T(8,128)S(1)}, f32[256,256]{1,0:T(8,128)}, u32[]{:S(2)}) copy-start(f32[256,256]{1,0:T(8,128)} %cx_ref.3) | copy-start | bytes 786436
  19.1 0.9 %copy-start.2 = (f32[256,256]{1,0:T(8,128)S(1)}, f32[256,256]{1,0:T(8,128)}, u32[]{:S(2)}) copy-start(f32[256,256]{1,0:T(8,128)} %cy_ref.3) | copy-start | bytes 786436
  62.6 20.2 %copy-start.1 = (f32[256,256]{1,0:T(8,128)S(1)}, f32[256,256]{1,0:T(8,128)}, u32[]{:S(2)}) copy-start(f32[256,256]{1,0:T(8,128)} %cx_ref.3) | copy-start | bytes 786436
  62.6 20.2 %copy-start.3 = (f32[256,256]{1,0:T(8,128)S(1)}, f32[256,256]{1,0:T(8,128)}, u32[]{:S(2)}) copy-start(f32[256,256]{1,0:T(8,128)} %cy_ref.3) | copy-start | bytes 786436
  70.3 5.1 %collective-permute-start = (f32[3,8,256]{2,1,0:T(8,128)S(1)}, f32[3,8,256]{2,1,0:T(8,128)S(1)}, u32[]{:S(2)}, u32[]{:S(2)}) collective-permute-start(f32[3,8,256]{2,1,0:T(8,128)S(1)} %get-tuple-element.22), channel_id=1, source_target_pairs={{0,1},{1,2},{2,3},{3,4},{4,5},{5,6},{6,7},{7,0},{8,9},{9,10},{10,1... | collective-permute-start | bytes 73736 | tf_op jit(solution)/shard_map/ppermute | solution.py:582
  70.3 5.1 %collective-permute-start.1 = (f32[3,8,256]{2,1,0:T(8,128)S(1)}, f32[3,8,256]{2,1,0:T(8,128)S(1)}, u32[]{:S(2)}, u32[]{:S(2)}) collective-permute-start(f32[3,8,256]{2,1,0:T(8,128)S(1)} %get-tuple-element.23), channel_id=1, source_target_pairs={{0,7},{1,0},{2,1},{3,2},{4,3},{5,4},{6,5},{7,6},{8,15},{9,8},{10,9... | collective-permute-start | bytes 73736 | tf_op jit(solution)/shard_map/ppermute | solution.py:583
  75.4 7.4 %collective-permute-start.2 = (f32[7,8,128]{2,1,0:T(8,128)S(1)}, f32[7,8,128]{2,1,0:T(8,128)S(1)}, u32[]{:S(2)}, u32[]{:S(2)}) collective-permute-start(f32[7,8,128]{2,1,0:T(8,128)S(1)} %pad_maximum_fusion), channel_id=1, source_target_pairs={{0,8},{8,16},{16,24},{24,32},{32,40},{40,48},{48,56},{56,64},{64,7... | collective-permute-start | bytes 86024 | tf_op jit(solution)/shard_map/ppermute | solution.py:586
  77.8 5.0 %collective-permute-start.3 = (f32[7,8,128]{2,1,0:T(8,128)S(1)}, f32[7,8,128]{2,1,0:T(8,128)S(1)}, u32[]{:S(2)}, u32[]{:S(2)}) collective-permute-start(f32[7,8,128]{2,1,0:T(8,128)S(1)} %pad_maximum_fusion.1), channel_id=1, source_target_pairs={{0,120},{8,0},{16,8},{24,16},{32,24},{40,32},{48,40},{56,48},{64,5... | collective-permute-start | bytes 86024 | tf_op jit(solution)/shard_map/ppermute | solution.py:587
where the time goes:
time: 90.3 us; the launch traced here: 89.8 us
  waiting for transfers between devices  43.8 us (49%)
  Pallas kernels  22.9 us (25%)
  starting transfers between devices  19.7 us (22%)
  local copies, waits for them, and re-layouts  1.92 us (2%)
  between operations  1.39 us (2%)
    all_to_all x1, waiting for transfers between devices, body(): lax.all_to_all(message.reshape(devices, SLOTS, 8, 128), ('gx', 'gy'), spl...  41.8 us
    all_to_all x1, starting transfers between devices, body(): lax.all_to_all(message.reshape(devices, SLOTS, 8, 128), ('gx', 'gy'), spl...  11.3 us
    pallas_call x1, Pallas kernels, bin_blocks(): pl.pallas_call(bin_kernel, out_shape=(shape(height + 1, 32, 128), shape(H...  7.67 us
    pallas_call x1, Pallas kernels, smooth(): pl.pallas_call(smooth_kernel, out_shape=(jax.ShapeDtypeStruct((6, height,...  6.98 us
    pallas_call x1, Pallas kernels, pack(): pl.pallas_call(pack_kernel, out_shape=(jax.ShapeDtypeStruct((devices * SL...  5.43 us
    ppermute x1, starting transfers between devices, body(): east = lax.ppermute(near, 'gx', ring(across, -1))  3.01 us
    ppermute x1, starting transfers between devices, body(): down = lax.ppermute(top, 'gy', ring(along, -1))  2.94 us
    ppermute x1, starting transfers between devices, body(): west = lax.ppermute(far, 'gx', ring(across, 1))  2.41 us
  transfers between devices with their start and end apart: 5, of which 2 were waited for; matrix products, arithmetic and copies ran while one was open for 0% of the time, Pallas kernels for 3%

commit v1 on v0

--- a/solution.py
+++ b/solution.py
@@ -69,7 +69,8 @@
     done_ref[...] = jnp.zeros((8, 128), f32)
     devices = out_ref.shape[0] // SLOTS
     live_count = count_ref[0]
-    earlier = (iota((blocks, blocks), 0) < iota((blocks, blocks), 1)).astype(f32).astype(bf16)
+    chunk = iota((128, 256), 1)
+    earlier = ((iota((128, 256), 0) < chunk) | (chunk >= 128)).astype(f32).astype(bf16)
 
     @pl.loop(0, devices // 2)
     def _(t):
@@ -81,7 +82,14 @@
     owner = jnp.where(live, owner, -1)
     named = (iota((devices, blocks), 0) == owner).astype(f32)
     named16 = named.astype(bf16)
-    before = jnp.dot(named16, earlier, preferred_element_type=f32)
+    before, seen = [], jnp.zeros((devices, 128), f32)
+    for first in range(0, blocks, 128):
+        found = jnp.dot(
+            named16[:, first : first + 128], earlier, preferred_element_type=f32
+        )
+        before.append(seen + found[:, 0:128])
+        seen = seen + found[:, 128:256]
+    before = jnp.concatenate(before, axis=1)
     rank = jnp.sum(named * before, axis=0, keepdims=True).astype(i32)
     slot_v[...] = jnp.where(live, owner * SLOTS + rank, CAPACITY)
     copy = pltpu.make_async_copy(slot_v, slot_s, sem)
@@ -216,8 +224,11 @@
 
     acc_ref[height] = jnp.zeros((32, 128), f32)
     copy.wait()
-    low_ids = iota((64, 128), 0).astype(f32)
-    quarter_ids = (iota((32, 128), 0) // 8).astype(f32)
+    ids = iota((16, 128), 0).astype(f32)
+    low_ids = [(ids + 16.0 * k).astype(bf16) for k in range(4)]
+    quarter_ids = [(2.0 * k + jnp.floor(ids * 0.125)).astype(bf16) for k in range(2)]
+    one = jnp.ones((16, 128), bf16)
+    zero = jnp.zeros((16, 128), bf16)
     empty = jnp.zeros((32, 128), bf16)
 
     @pl.loop(0, (lists_s[3, 0] + GROUP - 1) // GROUP)
@@ -227,16 +238,18 @@
             values, hits = [], []
             for i in range(2):
                 block = msg_ref[slot + i].astype(f32)
-                col = block[7:8, :]
-                quarter = jnp.where(
-                    col >= 128.0,
-                    jnp.where(col >= 192.0, 3.0, 2.0),
-                    jnp.where(col >= 64.0, 1.0, 0.0),
+                col = jnp.broadcast_to(block[7:8, :], (8, 128))
+                quarter = jnp.floor(col * (1.0 / 64.0))
+                low = col - 64.0 * quarter
+                block, quarter, low = (
+                    jnp.concatenate([x, x], axis=0).astype(bf16) for x in (block, quarter, low)
                 )
-                low = col - 64.0 * quarter
-                block4 = jnp.concatenate([block] * 4, axis=0)
-                values.append(jnp.where(quarter_ids == quarter, block4, 0.0).astype(bf16))
-                hits.append(jnp.where(low_ids == low, 1.0, 0.0).astype(bf16))
+                values.append(
+                    jnp.concatenate([jnp.where(q == quarter, block, zero) for q in quarter_ids], axis=0)
+                )
+                hits.append(
+                    jnp.concatenate([jnp.where(k == low, one, zero) for k in low_ids], axis=0)
+                )
             values = jnp.concatenate(
                 [
                     jnp.concatenate([values[0], empty], axis=1),
@@ -481,15 +494,16 @@
         before = [jnp.where(block == 0, up[1][h], before[h]) for h in range(2)]
         after = [jnp.where(block == steps - 1, down[0][h], after[h]) for h in range(2)]
         lines = [before] + lines + [after]
+        sides = [near[start + i] for i in range(ROWS + 2)]
         for i in range(ROWS):
             row = start + i + 1
             along_x, along_y = coefficients(start + i)
-            store(once, row, smooth_row(*lines[i : i + 3], near[row], along_x, along_y))
+            store(once, row, smooth_row(*lines[i : i + 3], sides[i + 1], along_x, along_y))
             inner = jnp.where(lane < 64, lines[i + 1][0], lines[i + 1][1])
             once_near[start + i] = relax(
-                near[row],
+                sides[i + 1],
                 inner + far[start + i],
-                near[row + 1] + near[row - 1],
+                sides[i + 2] + sides[i],
                 side_x[pl.ds(start + i, 1), :],
                 side_y[pl.ds(start + i, 1), :],
             )

time: 90.3 us -> 89.5 us (level)
  Pallas kernels: 22.9 us -> 21.6 us
    ppermute x1, starting transfers between devices: 2.41 us -> 0.08 us  [body(): west = lax.ppermute(far, 'gx', ring(across, 1))]
    ppermute x1, starting transfers between devices: 3.01 us -> 5.32 us  [body(): east = lax.ppermute(near, 'gx', ring(across, -1))]
    pallas_call x1, Pallas kernels: 7.67 us -> 6.24 us  [bin_blocks(): pl.pallas_call(bin_kernel, out_shape=(shape(height + 1, 32, 128), shape(H...]
where the time goes in v1:
time: 89.5 us; the launch traced here: 88.5 us
  waiting for transfers between devices  43.7 us (49%)
  Pallas kernels  21.6 us (24%)
  starting transfers between devices  19.8 us (22%)
  local copies, waits for them, and re-layouts  1.92 us (2%)
  between operations  1.41 us (2%)
    all_to_all x1, waiting for transfers between devices, body(): lax.all_to_all(message.reshape(devices, SLOTS, 8, 128), ('gx', 'gy'), spl...  41.8 us
    all_to_all x1, starting transfers between devices, body(): lax.all_to_all(message.reshape(devices, SLOTS, 8, 128), ('gx', 'gy'), spl...  11.4 us
    pallas_call x1, Pallas kernels, smooth(): pl.pallas_call(smooth_kernel, out_shape=(jax.ShapeDtypeStruct((6, height,...  6.98 us
    pallas_call x1, Pallas kernels, bin_blocks(): pl.pallas_call(bin_kernel, out_shape=(shape(height + 1, 32, 128), shape(H...  6.24 us
    pallas_call x1, Pallas kernels, pack(): pl.pallas_call(pack_kernel, out_shape=(jax.ShapeDtypeStruct((devices * SL...  5.51 us
    ppermute x1, starting transfers between devices, body(): east = lax.ppermute(near, 'gx', ring(across, -1))  5.32 us
    ppermute x1, starting transfers between devices, body(): down = lax.ppermute(top, 'gy', ring(along, -1))  2.94 us
    pallas_call x1, Pallas kernels, join(): pl.pallas_call(join_kernel, out_shape=(shape(height, 8, width), shape(hei...  2.12 us
  transfers between devices with their start and end apart: 5, of which 2 were waited for; matrix products, arithmetic and copies ran while one was open for 0% of the time, Pallas kernels for 3%

profile of v1, /device:TPU:0, one launch (start us, length us, event | category | flops | bytes accessed | tf_op | source)
XLA Modules:
  0.0 88.5 jit_solution(4805062129126394851)
XLA Ops:
  1.3 5.5 %pack.1 = (bf16[1664,8,128]{2,1,0:T(8,128)(2,1)}, f32[8,128]{1,0:T(8,128)}) custom-call(s32[1]{0:T(128)S(6)} %copy.10.count_ref, s32[1,1024]{1,0:T(1,128)} %bitcast.12, s32[1,1024]{1,0:T(1,128)} %bitcast.13, bf16[6,1024,128]{2,1,0:T(8,128)(2,1)} %bitcast.11, bf16[1024,128]{1,0:T(8,128)(2,1)} %weight_ref.1, s32[1024,128]{1,0:T(8,128)} %cols_ref.1), custom_call_target="tpu_custom_call" | custom-call | tf_op jit(solution)/shard_map/pack/pallas_call | solution.py:134
  6.8 0.0 copy-start.4
  6.8 11.4 %all-to-all-start = ((bf16[128,13,8,128]{3,2,1,0:T(8,128)(2,1)}), bf16[128,13,8,128]{3,2,1,0:T(8,128)(2,1)S(1)}, u32[]{:S(2)}, u32[]{:S(2)}) async-start(bf16[128,13,8,128]{3,2,1,0:T(8,128)(2,1)} %bitcast.10), calls=%async_computation | async-start | bytes 6815744 | tf_op jit(solution)/shard_map/all_to_all | solution.py:585
  18.2 0.1 add_convert_fusion.flags_ref
  18.3 0.0 copy-done.4
  18.3 0.0 copy-start
  18.3 1.0 %copy-done = f32[256,256]{1,0:T(8,128)S(1)} copy-done((f32[256,256]{1,0:T(8,128)S(1)}, f32[256,256]{1,0:T(8,128)}, u32[]{:S(2)}) %copy-start) | copy-done | bytes 262168
  19.3 0.0 copy-start.2
  19.3 0.9 %copy-done.2 = f32[256,256]{1,0:T(8,128)S(1)} copy-done((f32[256,256]{1,0:T(8,128)S(1)}, f32[256,256]{1,0:T(8,128)}, u32[]{:S(2)}) %copy-start.2) | copy-done | bytes 262168
  20.2 0.7 coefficient_edges.1
  21.0 41.8 %all-to-all-done = bf16[128,13,8,128]{3,2,1,0:T(8,128)(2,1)S(1)} async-done(((bf16[128,13,8,128]{3,2,1,0:T(8,128)(2,1)}), bf16[128,13,8,128]{3,2,1,0:T(8,128)(2,1)S(1)}, u32[]{:S(2)}, u32[]{:S(2)}) %all-to-all-start) | async-done | bytes 3407904 | tf_op jit(solution)/shard_map/all_to_all | solution.py:585
  62.8 0.0 copy-start.1
  62.8 0.0 copy-start.3
  62.8 6.2 %bin.1 = (f32[257,32,128]{2,1,0:T(8,128)S(1)}, f32[3,8,256]{2,1,0:T(8,128)S(1)}, f32[3,8,256]{2,1,0:T(8,128)S(1)}) custom-call(bf16[1664,8,128]{2,1,0:T(8,128)(2,1)S(1)} %bitcast.9, f32[8,256]{1,0:T(8,128)S(1)} %get-tuple-element.16.edge_top, f32[8,256]{1,0:T(8,128)S(1)} %get-tuple-element.17.edge_bottom), custom_call_target="tpu_custom_call" | custom-call | tf_op jit(solution)/shard_map/bin/pallas_call | solution.py:290
  69.0 0.0 collective-permute-start
  69.1 2.9 %collective-permute-start.1 = (f32[3,8,256]{2,1,0:T(8,128)S(1)}, f32[3,8,256]{2,1,0:T(8,128)S(1)}, u32[]{:S(2)}, u32[]{:S(2)}) collective-permute-start(f32[3,8,256]{2,1,0:T(8,128)S(1)} %get-tuple-element.23), channel_id=1, source_target_pairs={{0,7},{1,0},{2,1},{3,2},{4,3},{5,4},{6,5},{7,6},{8,15},{9,8},{10,9... | collective-permute-start | bytes 73736 | tf_op jit(solution)/shard_map/ppermute | solution.py:597
  72.0 2.1 %join.1 = (f32[256,8,256]{2,1,0:T(8,128)S(1)}, f32[5,8,128]{2,1,0:T(8,128)S(1)}, f32[5,8,128]{2,1,0:T(8,128)S(1)}) custom-call(f32[257,32,128]{2,1,0:T(8,128)S(1)} %get-tuple-element.18.acc_ref, f32[8,128]{1,0:T(8,128)S(1)} %get-tuple-element.19.edge_left, f32[8,128]{1,0:T(8,128)S(1)} %get-tuple-element.20.edge_right), custom_call_target="tpu_custom_call" | custom-call | tf_op jit(solution)/shard_map/join/pallas_call | solution.py:337
  74.1 0.0 collective-permute-done.up_ref
  74.2 0.0 collective-permute-done.1.down_ref
  74.2 0.1 collective-permute-start.2
  74.3 5.3 %collective-permute-start.3 = (f32[7,8,128]{2,1,0:T(8,128)S(1)}, f32[7,8,128]{2,1,0:T(8,128)S(1)}, u32[]{:S(2)}, u32[]{:S(2)}) collective-permute-start(f32[7,8,128]{2,1,0:T(8,128)S(1)} %pad_maximum_fusion.1), channel_id=1, source_target_pairs={{0,120},{8,0},{16,8},{24,16},{32,24},{40,32},{48,40},{56,48},{64,5... | collective-permute-start | bytes 86024 | tf_op jit(solution)/shard_map/ppermute | solution.py:601
  79.6 1.9 %collective-permute-done.2.west_ref = f32[7,8,128]{2,1,0:T(8,128)S(1)} collective-permute-done((f32[7,8,128]{2,1,0:T(8,128)S(1)}, f32[7,8,128]{2,1,0:T(8,128)S(1)}, u32[]{:S(2)}, u32[]{:S(2)}) %collective-permute-start.2) | collective-permute-done | bytes 28704 | tf_op jit(solution)/shard_map/ppermute | solution.py:600
  81.5 0.0 collective-permute-done.3.east_ref
  81.5 0.0 copy-done.1
  81.5 0.0 copy-done.3
  81.5 7.0 %smooth.1 = (f32[6,256,256]{2,1,0:T(8,128)}, f32[256,256]{1,0:T(8,128)}) custom-call(s32[4]{0:T(128)S(1)} %add_convert_fusion.flags_ref, f32[256,8,256]{2,1,0:T(8,128)S(1)} %get-tuple-element.21.acc_ref, f32[3,8,256]{2,1,0:T(8,128)S(1)} %collective-permute-done.up_ref, f32[3,8,256]{2,1,0:T(8,128)S(1)} %collective-permute-done.1.down_ref, ...), custom_call_target="tpu_custom_call" | custom-call | tf_op jit(solution)/shard_map/smooth/pallas_call | solution.py:515
  (4 shorter events, 0.0 us)
Async XLA Ops:
  6.8 11.5 %copy-start.4 = (f32[8,128]{1,0:T(8,128)S(1)}, f32[8,128]{1,0:T(8,128)}, u32[]{:S(2)}) copy-start(f32[8,128]{1,0:T(8,128)} %get-tuple-element.15.after_ref) | copy-start | bytes 12292
  6.8 56.0 %all-to-all-start = ((bf16[128,13,8,128]{3,2,1,0:T(8,128)(2,1)}), bf16[128,13,8,128]{3,2,1,0:T(8,128)(2,1)S(1)}, u32[]{:S(2)}, u32[]{:S(2)}) async-start(bf16[128,13,8,128]{3,2,1,0:T(8,128)(2,1)} %bitcast.10), calls=%async_computation | async-start | bytes 6815744 | tf_op jit(solution)/shard_map/all_to_all | solution.py:585
  18.3 1.0 %copy-start = (f32[256,256]{1,0:T(8,128)S(1)}, f32[256,256]{1,0:T(8,128)}, u32[]{:S(2)}) copy-start(f32[256,256]{1,0:T(8,128)} %cx_ref.3) | copy-start | bytes 786436
  19.3 0.9 %copy-start.2 = (f32[256,256]{1,0:T(8,128)S(1)}, f32[256,256]{1,0:T(8,128)}, u32[]{:S(2)}) copy-start(f32[256,256]{1,0:T(8,128)} %cy_ref.3) | copy-start | bytes 786436
  62.8 18.7 %copy-start.1 = (f32[256,256]{1,0:T(8,128)S(1)}, f32[256,256]{1,0:T(8,128)}, u32[]{:S(2)}) copy-start(f32[256,256]{1,0:T(8,128)} %cx_ref.3) | copy-start | bytes 786436
  62.8 18.7 %copy-start.3 = (f32[256,256]{1,0:T(8,128)S(1)}, f32[256,256]{1,0:T(8,128)}, u32[]{:S(2)}) copy-start(f32[256,256]{1,0:T(8,128)} %cy_ref.3) | copy-start | bytes 786436
  69.0 5.1 %collective-permute-start = (f32[3,8,256]{2,1,0:T(8,128)S(1)}, f32[3,8,256]{2,1,0:T(8,128)S(1)}, u32[]{:S(2)}, u32[]{:S(2)}) collective-permute-start(f32[3,8,256]{2,1,0:T(8,128)S(1)} %get-tuple-element.22), channel_id=1, source_target_pairs={{0,1},{1,2},{2,3},{3,4},{4,5},{5,6},{6,7},{7,0},{8,9},{9,10},{10,1... | collective-permute-start | bytes 73736 | tf_op jit(solution)/shard_map/ppermute | solution.py:596
  69.1 5.1 %collective-permute-start.1 = (f32[3,8,256]{2,1,0:T(8,128)S(1)}, f32[3,8,256]{2,1,0:T(8,128)S(1)}, u32[]{:S(2)}, u32[]{:S(2)}) collective-permute-start(f32[3,8,256]{2,1,0:T(8,128)S(1)} %get-tuple-element.23), channel_id=1, source_target_pairs={{0,7},{1,0},{2,1},{3,2},{4,3},{5,4},{6,5},{7,6},{8,15},{9,8},{10,9... | collective-permute-start | bytes 73736 | tf_op jit(solution)/shard_map/ppermute | solution.py:597
  74.2 7.3 %collective-permute-start.2 = (f32[7,8,128]{2,1,0:T(8,128)S(1)}, f32[7,8,128]{2,1,0:T(8,128)S(1)}, u32[]{:S(2)}, u32[]{:S(2)}) collective-permute-start(f32[7,8,128]{2,1,0:T(8,128)S(1)} %pad_maximum_fusion), channel_id=1, source_target_pairs={{0,8},{8,16},{16,24},{24,32},{32,40},{40,48},{48,56},{56,64},{64,7... | collective-permute-start | bytes 86024 | tf_op jit(solution)/shard_map/ppermute | solution.py:600
  74.3 7.2 %collective-permute-start.3 = (f32[7,8,128]{2,1,0:T(8,128)S(1)}, f32[7,8,128]{2,1,0:T(8,128)S(1)}, u32[]{:S(2)}, u32[]{:S(2)}) collective-permute-start(f32[7,8,128]{2,1,0:T(8,128)S(1)} %pad_maximum_fusion.1), channel_id=1, source_target_pairs={{0,120},{8,0},{16,8},{24,16},{32,24},{40,32},{48,40},{56,48},{64,5... | collective-permute-start | bytes 86024 | tf_op jit(solution)/shard_map/ppermute | solution.py:601

commit v2 on v1

--- a/solution.py
+++ b/solution.py
@@ -307,23 +307,21 @@
     )(message, edge_top, edge_bottom)
 
 
-def join_kernel(acc_ref, edge_left, edge_right, fields_ref, left_ref, right_ref):
+def strip_kernel(acc_ref, edge_left, edge_right, left_ref, right_ref):
     lane = iota((8, 128), 1)
     blank = jnp.zeros((8, 128), f32)
 
-    def join_rows(j, carry):
+    def take(j, carry):
         here = lane // 2 == j
         result = []
         for q in range(4):
-            row = q * 64 + j
-            first, last = join_quarters(acc_ref[row])
-            fields_ref[row, :, 0:128] = first
-            fields_ref[row, :, 128:256] = last
-            result.append(jnp.where(here, pltpu.roll(first, 2 * j, 1), carry[2 * q]))
-            result.append(jnp.where(here, pltpu.roll(last, 2 * j + 2, 1), carry[2 * q + 1]))
+            first = pltpu.roll(acc_ref[q * 64 + j, 0:8], 2 * j, 1)
+            last = pltpu.roll(acc_ref[q * 64 + j, 24:32], (2 * j + 66) % 128, 1)
+            result.append(jnp.where(here, first, carry[2 * q]))
+            result.append(jnp.where(here, last, carry[2 * q + 1]))
         return tuple(result)
 
-    strips = lax.fori_loop(0, 64, join_rows, (blank,) * 8, unroll=8)
+    strips = lax.fori_loop(0, 64, take, (blank,) * 8, unroll=8)
     for q in range(4):
         left_ref[q] = strips[2 * q]
         right_ref[q] = strips[2 * q + 1]
@@ -331,20 +329,16 @@
     right_ref[4] = edge_right[...]
 
 
-def join(acc, edge_left, edge_right, height, width):
+def column_strips(acc, edge_left, edge_right):
     vmem = pl.BlockSpec(memory_space=pltpu.VMEM)
-    shape = lambda *dims: jax.ShapeDtypeStruct(dims, f32)
+    strip = jax.ShapeDtypeStruct(((acc.shape[0] - 1) // 64 + 1, 8, 128), f32)
     return pl.pallas_call(
-        join_kernel,
-        out_shape=(
-            shape(height, 8, width),
-            shape(height // 64 + 1, 8, 128),
-            shape(height // 64 + 1, 8, 128),
-        ),
+        strip_kernel,
+        out_shape=(strip, strip),
         in_specs=[vmem] * 3,
-        out_specs=(vmem,) * 3,
+        out_specs=(vmem,) * 2,
         compiler_params=pltpu.CompilerParams(vmem_limit_bytes=12 << 20),
-        name="join",
+        name="column_strips",
     )(acc, edge_left, edge_right)
 
 
@@ -364,9 +358,87 @@
     ]
 
 
-def smooth_kernel(
+def halves(ref, row):
+    return [ref[row, :, 0:128], ref[row, :, 128:256]]
+
+
+def keep(flag, parts):
+    return [jnp.where(flag, part, 0.0) for part in parts]
+
+
+def line(ref, row):
+    both = ref[pl.ds(row, 1), :]
+    return [both[:, 0:128], both[:, 128:256]]
+
+
+def beyond(ref, flag):
+    return [
+        keep(flag, [ref[HALO, i : i + 1, h * 128 : h * 128 + 128] for h in range(2)])
+        for i in range(2)
+    ]
+
+
+def first_kernel(flags_ref, acc_ref, up_ref, down_ref, cx_ref, cy_ref, once_ref, inner_ref):
+    height = inner_ref.shape[0]
+    has_up, has_down = flags_ref[0] > 0, flags_ref[1] > 0
+    lane = iota((8, 128), 1)
+    blank = jnp.zeros((8, 128), f32)
+    up = [keep(has_up, halves(up_ref, i)) for i in range(2)]
+    down = [keep(has_down, halves(down_ref, i)) for i in range(2)]
+
+    def store(row, parts):
+        once_ref[row, :, 0:128] = parts[0]
+        once_ref[row, :, 128:256] = parts[1]
+
+    store(0, smooth_row(up[0], up[1], join_quarters(acc_ref[0]), blank, *beyond(up_ref, has_up)))
+    store(
+        height + 1,
+        smooth_row(
+            join_quarters(acc_ref[height - 1]),
+            down[0],
+            down[1],
+            blank,
+            *beyond(down_ref, has_down),
+        ),
+    )
+    steps = height // ROWS
+
+    @pl.loop(0, steps)
+    def _(block):
+        start = block * ROWS
+        before = join_quarters(acc_ref[jnp.maximum(start - 1, 0)])
+        after = join_quarters(acc_ref[jnp.minimum(start + ROWS, height - 1)])
+        before = [jnp.where(block == 0, up[1][h], before[h]) for h in range(2)]
+        after = [jnp.where(block == steps - 1, down[0][h], after[h]) for h in range(2)]
+        lines = [before] + [join_quarters(acc_ref[start + i]) for i in range(ROWS)] + [after]
+        for i in range(ROWS):
+            fresh = smooth_row(
+                *lines[i : i + 3], blank, line(cx_ref, start + i), line(cy_ref, start + i)
+            )
+            store(start + i + 1, fresh)
+            inner_ref[start + i] = jnp.where(lane < 64, lines[i + 1][0], lines[i + 1][1])
+
+
+def first_pass(flags, acc, up, down, cx, cy):
+    height, width = cx.shape
+    vmem = pl.BlockSpec(memory_space=pltpu.VMEM)
+    return pl.pallas_call(
+        first_kernel,
+        out_shape=(
+            jax.ShapeDtypeStruct((height + 2, 8, width), f32),
+            jax.ShapeDtypeStruct((height, 8, 128), f32),
+        ),
+        in_specs=[pl.BlockSpec(memory_space=pltpu.SMEM)] + [vmem] * 5,
+        out_specs=(vmem, vmem),
+        compiler_params=pltpu.CompilerParams(vmem_limit_bytes=20 << 20),
+        name="first_pass",
+    )(flags, acc, up, down, cx, cy)
+
+
+def second_kernel(
     flags_ref,
-    acc_ref,
+    once_ref,
+    inner_ref,
     up_ref,
     down_ref,
     west_ref,
@@ -379,26 +451,14 @@
     mix_far,
     near,
     far,
-    once,
-    once_near,
     twice,
     side_x,
     side_y,
 ):
-    height, _, width = acc_ref.shape
+    height, width = cx_ref.shape
     has_up, has_down = flags_ref[0] > 0, flags_ref[1] > 0
     has_west, has_east = flags_ref[2] > 0, flags_ref[3] > 0
     lane = iota((8, 128), 1)
-
-    def halves(ref, row):
-        return [ref[row, :, 0:128], ref[row, :, 128:256]]
-
-    def keep(flag, parts):
-        return [jnp.where(flag, part, 0.0) for part in parts]
-
-    def along(ref, row):
-        line = ref[pl.ds(row, 1), :]
-        return [line[:, i : i + 128] for i in (0, 128)]
 
     for q in range(4):
         west = jnp.where(has_west, west_ref[q], 0.0)
@@ -429,43 +489,20 @@
             )
             side[half * 128 : half * 128 + 128, :] = both.T
 
-    up = [keep(has_up, halves(up_ref, i)) for i in range(2)]
-    down = [keep(has_down, halves(down_ref, i)) for i in range(2)]
-
-    def store(ref, row, parts):
-        ref[row, :, 0:128] = parts[0]
-        ref[row, :, 128:256] = parts[1]
-
-    def coefficients(row):
-        return along(cx_ref, row), along(cy_ref, row)
-
-    def beyond(ref, flag):
+    above_x = beyond(up_ref, has_up)[0]
+    below_x = beyond(down_ref, has_down)[0]
+    steps = height // ROWS
+
+    def completed(row, beside, along_x):
+        first, last = halves(once_ref, row)
         return [
-            keep(flag, [ref[HALO, i : i + 1, h * 128 : h * 128 + 128] for h in range(2)])
-            for i in range(2)
+            first + jnp.where(lane == 0, along_x[0] * beside, 0.0),
+            last + jnp.where(lane == 127, along_x[1] * beside, 0.0),
         ]
 
-    store(
-        once,
-        0,
-        smooth_row(up[0], up[1], halves(acc_ref, 0), near[0], *beyond(up_ref, has_up)),
-    )
-    store(
-        once,
-        height + 1,
-        smooth_row(
-            halves(acc_ref, height - 1),
-            down[0],
-            down[1],
-            near[height + 1],
-            *beyond(down_ref, has_down),
-        ),
-    )
-    steps = height // ROWS
-
-    @pl.loop(0, steps + 3)
+    @pl.loop(0, steps + 1)
     def _(g):
-        block = jnp.clip(g - 3, 0, steps - 1)
+        block = jnp.maximum(g - 1, 0)
         for part in range(ROWS // 8):
             base = block * ROWS + part * 8
             rows = pl.ds(pl.multiple_of(base, 8), 8)
@@ -478,62 +515,53 @@
                     gridded_ref[c, rows, cols] = (
                         twice[half, pl.ds(base * 8 + c, 8, stride=8), :] * scale
                     )
-        start = jnp.clip(g - 2, 0, steps - 1) * ROWS
-        lines = [halves(once, start + i) for i in range(ROWS + 2)]
-        for i in range(ROWS):
-            fresh = smooth_row(
-                *lines[i : i + 3], once_near[start + i], *coefficients(start + i)
-            )
-            for half in range(2):
-                twice[half, pl.ds(pl.multiple_of((start + i) * 8, 8), 8), :] = fresh[half]
         block = jnp.minimum(g, steps - 1)
         start = block * ROWS
-        lines = [halves(acc_ref, start + i) for i in range(ROWS)]
-        before = halves(acc_ref, jnp.maximum(start - 1, 0))
-        after = halves(acc_ref, jnp.minimum(start + ROWS, height - 1))
-        before = [jnp.where(block == 0, up[1][h], before[h]) for h in range(2)]
-        after = [jnp.where(block == steps - 1, down[0][h], after[h]) for h in range(2)]
-        lines = [before] + lines + [after]
         sides = [near[start + i] for i in range(ROWS + 2)]
+        along_x = [line(cx_ref, start + i) for i in range(ROWS)]
+        along_y = [line(cy_ref, start + i) for i in range(ROWS)]
+        before = line(cx_ref, jnp.maximum(start - 1, 0))
+        after = line(cx_ref, jnp.minimum(start + ROWS, height - 1))
+        before = [jnp.where(block == 0, above_x[h], before[h]) for h in range(2)]
+        after = [jnp.where(block == steps - 1, below_x[h], after[h]) for h in range(2)]
+        factors = [before] + along_x + [after]
+        lines = [completed(start + i, sides[i], factors[i]) for i in range(ROWS + 2)]
         for i in range(ROWS):
-            row = start + i + 1
-            along_x, along_y = coefficients(start + i)
-            store(once, row, smooth_row(*lines[i : i + 3], sides[i + 1], along_x, along_y))
-            inner = jnp.where(lane < 64, lines[i + 1][0], lines[i + 1][1])
-            once_near[start + i] = relax(
+            beside = relax(
                 sides[i + 1],
-                inner + far[start + i],
+                inner_ref[start + i] + far[start + i],
                 sides[i + 2] + sides[i],
                 side_x[pl.ds(start + i, 1), :],
                 side_y[pl.ds(start + i, 1), :],
             )
-
-
-def smooth(flags, acc, up, down, west, east, cx, cy):
-    height, _, width = acc.shape
+            fresh = smooth_row(*lines[i : i + 3], beside, along_x[i], along_y[i])
+            for half in range(2):
+                twice[half, pl.ds(pl.multiple_of((start + i) * 8, 8), 8), :] = fresh[half]
+
+
+def second_pass(flags, once, inner, up, down, west, east, cx, cy):
+    height, width = cx.shape
     vmem = pl.BlockSpec(memory_space=pltpu.VMEM)
     return pl.pallas_call(
-        smooth_kernel,
+        second_kernel,
         out_shape=(
             jax.ShapeDtypeStruct((6, height, width), f32),
             jax.ShapeDtypeStruct((height, width), f32),
         ),
-        in_specs=[pl.BlockSpec(memory_space=pltpu.SMEM)] + [vmem] * 7,
+        in_specs=[pl.BlockSpec(memory_space=pltpu.SMEM)] + [vmem] * 8,
         out_specs=(vmem, vmem),
         scratch_shapes=[
             pltpu.VMEM((4, 8, 128), f32),
             pltpu.VMEM((4, 8, 128), f32),
             pltpu.VMEM((height + 2, 8, 128), f32),
             pltpu.VMEM((height, 8, 128), f32),
-            pltpu.VMEM((height + 2, 8, width), f32),
-            pltpu.VMEM((height, 8, 128), f32),
             pltpu.VMEM((width // 128, height * 8, 128), f32),
             pltpu.VMEM((height, 128), f32),
             pltpu.VMEM((height, 128), f32),
         ],
         compiler_params=pltpu.CompilerParams(vmem_limit_bytes=24 << 20),
-        name="smooth",
-    )(flags, acc, up, down, west, east, cx, cy)
+        name="second_pass",
+    )(flags, once, inner, up, down, west, east, cx, cy)
 
 
 def edge_kernel(after_ref, flags_ref, cx_ref, cy_ref, top_ref, bottom_ref, left_ref, right_ref):
@@ -592,14 +620,15 @@
 
     edges = coefficient_edges(packed, flags, conduct_x, conduct_y)
     acc, top, bottom = bin_blocks(arrived, edges[0], edges[1], height, width)
-    fields, left, right = join(acc, edges[2], edges[3], height, width)
+    left, right = column_strips(acc, edges[2], edges[3])
     up = lax.ppermute(bottom, "gy", ring(along, 1))
     down = lax.ppermute(top, "gy", ring(along, -1))
     near = jnp.concatenate([left, up[1:2, :, 0:128], down[0:1, :, 0:128]], axis=0)
     far = jnp.concatenate([right, up[1:2, :, width - 128 :], down[0:1, :, width - 128 :]], axis=0)
     west = lax.ppermute(far, "gx", ring(across, 1))
     east = lax.ppermute(near, "gx", ring(across, -1))
-    return smooth(flags, fields, up, down, west, east, conduct_x, conduct_y)
+    once, inner = first_pass(flags, acc, up, down, conduct_x, conduct_y)
+    return second_pass(flags, once, inner, up, down, west, east, conduct_x, conduct_y)
 
 
 def solution(mesh):

time: 89.5 us -> 90.7 us (1.013)
  Pallas kernels: 21.6 us -> 24.6 us
  waiting for transfers between devices: 43.7 us -> 42.2 us
    ppermute x1, waiting for transfers between devices: 1.91 us -> 0.01 us  [body(): west = lax.ppermute(far, 'gx', ring(across, 1))]
    pallas_call x2 -> x3, Pallas kernels: 9.1 us -> 10.7 us  [the longest x1 5.65 us: second_pass(): pl.pallas_call(second_kernel, out_shape=(jax.ShapeDtypeStruct((6, height,...]
    pallas_call x1, Pallas kernels: 6.24 us -> 7.67 us  [bin_blocks(): pl.pallas_call(bin_kernel, out_shape=(shape(height + 1, 32, 128), shape(H...]
  transfers between devices with their start and end apart: 5 -> 5, of which waited for: 2 -> 2; matrix products, arithmetic and copies ran while one was open for 0% -> 0% of each run, Pallas kernels for 3% -> 6%
where the time goes in v2:
time: 90.7 us; the launch traced here: 90 us
  waiting for transfers between devices  42.2 us (47%)
  Pallas kernels  24.6 us (27%)
  starting transfers between devices  19.8 us (22%)
  local copies, waits for them, and re-layouts  1.92 us (2%)
  between operations  1.39 us (2%)
    all_to_all x1, waiting for transfers between devices, body(): lax.all_to_all(message.reshape(devices, SLOTS, 8, 128), ('gx', 'gy'), spl...  41.8 us
    all_to_all x1, starting transfers between devices, body(): lax.all_to_all(message.reshape(devices, SLOTS, 8, 128), ('gx', 'gy'), spl...  11.4 us
    pallas_call x1, Pallas kernels, bin_blocks(): pl.pallas_call(bin_kernel, out_shape=(shape(height + 1, 32, 128), shape(H...  7.67 us
    pallas_call x1, Pallas kernels, second_pass(): pl.pallas_call(second_kernel, out_shape=(jax.ShapeDtypeStruct((6, height,...  5.65 us
    pallas_call x1, Pallas kernels, pack(): pl.pallas_call(pack_kernel, out_shape=(jax.ShapeDtypeStruct((devices * SL...  5.49 us
    ppermute x1, starting transfers between devices, body(): east = lax.ppermute(near, 'gx', ring(across, -1))  5.32 us
    pallas_call x1, Pallas kernels, first_pass(): pl.pallas_call(first_kernel, out_shape=(jax.ShapeDtypeStruct((height + 2,...  3.99 us
    ppermute x1, starting transfers between devices, body(): down = lax.ppermute(top, 'gy', ring(along, -1))  2.94 us
  transfers between devices with their start and end apart: 5, of which 2 were waited for; matrix products, arithmetic and copies ran while one was open for 0% of the time, Pallas kernels for 6%

profile of v2, /device:TPU:0, one launch (start us, length us, event | category | flops | bytes accessed | tf_op | source)
XLA Modules:
  0.0 90.0 jit_solution(9441466432321375705)
XLA Ops:
  1.3 5.5 %pack.1 = (bf16[1664,8,128]{2,1,0:T(8,128)(2,1)}, f32[8,128]{1,0:T(8,128)}) custom-call(s32[1]{0:T(128)S(6)} %copy.10.count_ref, s32[1,1024]{1,0:T(1,128)} %bitcast.12, s32[1,1024]{1,0:T(1,128)} %bitcast.13, bf16[6,1024,128]{2,1,0:T(8,128)(2,1)} %bitcast.11, bf16[1024,128]{1,0:T(8,128)(2,1)} %weight_ref.1, s32[1024,128]{1,0:T(8,128)} %cols_ref.1), custom_call_target="tpu_custom_call" | custom-call | tf_op jit(solution)/shard_map/pack/pallas_call | solution.py:134
  6.8 0.0 copy-start.4
  6.8 11.4 %all-to-all-start = ((bf16[128,13,8,128]{3,2,1,0:T(8,128)(2,1)}), bf16[128,13,8,128]{3,2,1,0:T(8,128)(2,1)S(1)}, u32[]{:S(2)}, u32[]{:S(2)}) async-start(bf16[128,13,8,128]{3,2,1,0:T(8,128)(2,1)} %bitcast.10), calls=%async_computation | async-start | bytes 6815744 | tf_op jit(solution)/shard_map/all_to_all | solution.py:613
  18.2 0.1 add_convert_fusion.flags_ref
  18.3 0.0 copy-done.4
  18.3 0.0 copy-start
  18.3 1.0 %copy-done = f32[256,256]{1,0:T(8,128)S(1)} copy-done((f32[256,256]{1,0:T(8,128)S(1)}, f32[256,256]{1,0:T(8,128)}, u32[]{:S(2)}) %copy-start) | copy-done | bytes 262168
  19.3 0.0 copy-start.2
  19.3 0.9 %copy-done.2 = f32[256,256]{1,0:T(8,128)S(1)} copy-done((f32[256,256]{1,0:T(8,128)S(1)}, f32[256,256]{1,0:T(8,128)}, u32[]{:S(2)}) %copy-start.2) | copy-done | bytes 262168
  20.2 0.7 coefficient_edges.1
  21.0 41.8 %all-to-all-done = bf16[128,13,8,128]{3,2,1,0:T(8,128)(2,1)S(1)} async-done(((bf16[128,13,8,128]{3,2,1,0:T(8,128)(2,1)}), bf16[128,13,8,128]{3,2,1,0:T(8,128)(2,1)S(1)}, u32[]{:S(2)}, u32[]{:S(2)}) %all-to-all-start) | async-done | bytes 3407904 | tf_op jit(solution)/shard_map/all_to_all | solution.py:613
  62.8 0.0 copy-start.1
  62.8 0.0 copy-start.3
  62.8 7.7 %bin.1 = (f32[257,32,128]{2,1,0:T(8,128)S(1)}, f32[3,8,256]{2,1,0:T(8,128)S(1)}, f32[3,8,256]{2,1,0:T(8,128)S(1)}) custom-call(bf16[1664,8,128]{2,1,0:T(8,128)(2,1)S(1)} %bitcast.9, f32[8,256]{1,0:T(8,128)S(1)} %get-tuple-element.17.edge_top, f32[8,256]{1,0:T(8,128)S(1)} %get-tuple-element.18.edge_bottom), custom_call_target="tpu_custom_call" | custom-call | tf_op jit(solution)/shard_map/bin/pallas_call | solution.py:290
  70.5 0.0 collective-permute-start
  70.5 2.9 %collective-permute-start.1 = (f32[3,8,256]{2,1,0:T(8,128)S(1)}, f32[3,8,256]{2,1,0:T(8,128)S(1)}, u32[]{:S(2)}, u32[]{:S(2)}) collective-permute-start(f32[3,8,256]{2,1,0:T(8,128)S(1)} %get-tuple-element.21), channel_id=1, source_target_pairs={{0,7},{1,0},{2,1},{3,2},{4,3},{5,4},{6,5},{7,6},{8,15},{9,8},{10,9... | collective-permute-start | bytes 73736 | tf_op jit(solution)/shard_map/ppermute | solution.py:625
  73.4 1.1 %column_strips.1 = (f32[5,8,128]{2,1,0:T(8,128)S(1)}, f32[5,8,128]{2,1,0:T(8,128)S(1)}) custom-call(f32[257,32,128]{2,1,0:T(8,128)S(1)} %get-tuple-element.19.acc_ref, f32[8,128]{1,0:T(8,128)S(1)} %get-tuple-element.24.edge_left, f32[8,128]{1,0:T(8,128)S(1)} %get-tuple-element.25.edge_right), custom_call_target="tpu_custom_call" | custom-call | tf_op jit(solution)/shard_map/column_strips/pallas_call | solution.py:335
  74.5 0.4 collective-permute-done.up_ref
  74.9 0.0 collective-permute-done.1.down_ref
  75.0 0.1 collective-permute-start.2
  75.0 5.3 %collective-permute-start.3 = (f32[7,8,128]{2,1,0:T(8,128)S(1)}, f32[7,8,128]{2,1,0:T(8,128)S(1)}, u32[]{:S(2)}, u32[]{:S(2)}) collective-permute-start(f32[7,8,128]{2,1,0:T(8,128)S(1)} %pad_maximum_fusion.1), channel_id=1, source_target_pairs={{0,120},{8,0},{16,8},{24,16},{32,24},{40,32},{48,40},{56,48},{64,5... | collective-permute-start | bytes 86024 | tf_op jit(solution)/shard_map/ppermute | solution.py:629
  80.4 0.0 copy-done.1
  80.4 0.0 copy-done.3
  80.4 4.0 %first_pass.1 = (f32[258,8,256]{2,1,0:T(8,128)S(1)}, f32[256,8,128]{2,1,0:T(8,128)S(1)}) custom-call(s32[4]{0:T(128)S(1)} %add_convert_fusion.flags_ref, f32[257,32,128]{2,1,0:T(8,128)S(1)} %get-tuple-element.19.acc_ref, f32[3,8,256]{2,1,0:T(8,128)S(1)} %collective-permute-done.up_ref, f32[3,8,256]{2,1,0:T(8,128)S(1)} %collective-permute-done.1.down_ref, ...), custom_call_target="tpu_custom_call" | custom-call | tf_op jit(solution)/shard_map/first_pass/pallas_call | solution.py:425
  84.4 0.0 collective-permute-done.2.west_ref
  84.4 0.0 collective-permute-done.3.east_ref
  84.4 5.7 %second_pass.1 = (f32[6,256,256]{2,1,0:T(8,128)}, f32[256,256]{1,0:T(8,128)}) custom-call(s32[4]{0:T(128)S(1)} %add_convert_fusion.flags_ref, f32[258,8,256]{2,1,0:T(8,128)S(1)} %get-tuple-element.22.once_ref, f32[256,8,128]{2,1,0:T(8,128)S(1)} %get-tuple-element.23.inner_ref, f32[3,8,256]{2,1,0:T(8,128)S(1)} %collective-permute-done.up_ref, ...), custom_call_target="tpu_custom_call" | custom-call | tf_op jit(solution)/shard_map/second_pass/pallas_call | solution.py:545
  (4 shorter events, 0.0 us)
Async XLA Ops:
  6.8 11.6 %copy-start.4 = (f32[8,128]{1,0:T(8,128)S(1)}, f32[8,128]{1,0:T(8,128)}, u32[]{:S(2)}) copy-start(f32[8,128]{1,0:T(8,128)} %get-tuple-element.16.after_ref) | copy-start | bytes 12292
  6.8 56.0 %all-to-all-start = ((bf16[128,13,8,128]{3,2,1,0:T(8,128)(2,1)}), bf16[128,13,8,128]{3,2,1,0:T(8,128)(2,1)S(1)}, u32[]{:S(2)}, u32[]{:S(2)}) async-start(bf16[128,13,8,128]{3,2,1,0:T(8,128)(2,1)} %bitcast.10), calls=%async_computation | async-start | bytes 6815744 | tf_op jit(solution)/shard_map/all_to_all | solution.py:613
  18.3 1.0 %copy-start = (f32[256,256]{1,0:T(8,128)S(1)}, f32[256,256]{1,0:T(8,128)}, u32[]{:S(2)}) copy-start(f32[256,256]{1,0:T(8,128)} %cx_ref.5) | copy-start | bytes 786436
  19.3 0.9 %copy-start.2 = (f32[256,256]{1,0:T(8,128)S(1)}, f32[256,256]{1,0:T(8,128)}, u32[]{:S(2)}) copy-start(f32[256,256]{1,0:T(8,128)} %cy_ref.5) | copy-start | bytes 786436
  62.8 17.6 %copy-start.1 = (f32[256,256]{1,0:T(8,128)S(1)}, f32[256,256]{1,0:T(8,128)}, u32[]{:S(2)}) copy-start(f32[256,256]{1,0:T(8,128)} %cx_ref.5) | copy-start | bytes 786436
  62.8 17.6 %copy-start.3 = (f32[256,256]{1,0:T(8,128)S(1)}, f32[256,256]{1,0:T(8,128)}, u32[]{:S(2)}) copy-start(f32[256,256]{1,0:T(8,128)} %cy_ref.5) | copy-start | bytes 786436
  70.5 4.5 %collective-permute-start = (f32[3,8,256]{2,1,0:T(8,128)S(1)}, f32[3,8,256]{2,1,0:T(8,128)S(1)}, u32[]{:S(2)}, u32[]{:S(2)}) collective-permute-start(f32[3,8,256]{2,1,0:T(8,128)S(1)} %get-tuple-element.20), channel_id=1, source_target_pairs={{0,1},{1,2},{2,3},{3,4},{4,5},{5,6},{6,7},{7,0},{8,9},{9,10},{10,1... | collective-permute-start | bytes 73736 | tf_op jit(solution)/shard_map/ppermute | solution.py:624
  70.5 4.5 %collective-permute-start.1 = (f32[3,8,256]{2,1,0:T(8,128)S(1)}, f32[3,8,256]{2,1,0:T(8,128)S(1)}, u32[]{:S(2)}, u32[]{:S(2)}) collective-permute-start(f32[3,8,256]{2,1,0:T(8,128)S(1)} %get-tuple-element.21), channel_id=1, source_target_pairs={{0,7},{1,0},{2,1},{3,2},{4,3},{5,4},{6,5},{7,6},{8,15},{9,8},{10,9... | collective-permute-start | bytes 73736 | tf_op jit(solution)/shard_map/ppermute | solution.py:625
  75.0 9.4 %collective-permute-start.2 = (f32[7,8,128]{2,1,0:T(8,128)S(1)}, f32[7,8,128]{2,1,0:T(8,128)S(1)}, u32[]{:S(2)}, u32[]{:S(2)}) collective-permute-start(f32[7,8,128]{2,1,0:T(8,128)S(1)} %pad_maximum_fusion), channel_id=1, source_target_pairs={{0,8},{8,16},{16,24},{24,32},{32,40},{40,48},{48,56},{56,64},{64,7... | collective-permute-start | bytes 86024 | tf_op jit(solution)/shard_map/ppermute | solution.py:628
  75.0 9.3 %collective-permute-start.3 = (f32[7,8,128]{2,1,0:T(8,128)S(1)}, f32[7,8,128]{2,1,0:T(8,128)S(1)}, u32[]{:S(2)}, u32[]{:S(2)}) collective-permute-start(f32[7,8,128]{2,1,0:T(8,128)S(1)} %pad_maximum_fusion.1), channel_id=1, source_target_pairs={{0,120},{8,0},{16,8},{24,16},{32,24},{40,32},{48,40},{56,48},{64,5... | collective-permute-start | bytes 86024 | tf_op jit(solution)/shard_map/ppermute | solution.py:629

commit v3 on v2

--- a/solution.py
+++ b/solution.py
@@ -13,7 +13,8 @@
 CODES = 16
 ENTRIES = 896
 GROUP = 64
-ROWS = 16
+FIRST_ROWS = 64
+ROWS = 32
 FLOOR = 0.15
 HALO = 2
 
@@ -401,17 +402,17 @@
             *beyond(down_ref, has_down),
         ),
     )
-    steps = height // ROWS
+    steps = height // FIRST_ROWS
 
     @pl.loop(0, steps)
     def _(block):
-        start = block * ROWS
+        start = block * FIRST_ROWS
         before = join_quarters(acc_ref[jnp.maximum(start - 1, 0)])
-        after = join_quarters(acc_ref[jnp.minimum(start + ROWS, height - 1)])
+        after = join_quarters(acc_ref[jnp.minimum(start + FIRST_ROWS, height - 1)])
         before = [jnp.where(block == 0, up[1][h], before[h]) for h in range(2)]
         after = [jnp.where(block == steps - 1, down[0][h], after[h]) for h in range(2)]
-        lines = [before] + [join_quarters(acc_ref[start + i]) for i in range(ROWS)] + [after]
-        for i in range(ROWS):
+        lines = [before] + [join_quarters(acc_ref[start + i]) for i in range(FIRST_ROWS)] + [after]
+        for i in range(FIRST_ROWS):
             fresh = smooth_row(
                 *lines[i : i + 3], blank, line(cx_ref, start + i), line(cy_ref, start + i)
             )

time: 90.7 us -> 88.2 us (0.972)
  Pallas kernels: 24.6 us -> 20.6 us
    pallas_call x1, Pallas kernels: 7.67 us -> 6.24 us  [bin_blocks(): pl.pallas_call(bin_kernel, out_shape=(shape(height + 1, 32, 128), shape(H...]
    pallas_call x1, Pallas kernels: 3.99 us -> 2.57 us  [first_pass(): pl.pallas_call(first_kernel, out_shape=(jax.ShapeDtypeStruct((height + 2,...]
  transfers between devices with their start and end apart: 5 -> 5, of which waited for: 2 -> 2; matrix products, arithmetic and copies ran while one was open for 0% -> 0% of each run, Pallas kernels for 6% -> 5%
where the time goes in v3:
time: 88.2 us; the launch traced here: 86.7 us
  waiting for transfers between devices  42.2 us (48%)
  Pallas kernels  20.6 us (23%)
  starting transfers between devices  20.4 us (23%)
  local copies, waits for them, and re-layouts  1.92 us (2%)
  between operations  1.39 us (2%)
    all_to_all x1, waiting for transfers between devices, body(): lax.all_to_all(message.reshape(devices, SLOTS, 8, 128), ('gx', 'gy'), spl...  41.8 us
    all_to_all x1, starting transfers between devices, body(): lax.all_to_all(message.reshape(devices, SLOTS, 8, 128), ('gx', 'gy'), spl...  12.1 us
    pallas_call x1, Pallas kernels, bin_blocks(): pl.pallas_call(bin_kernel, out_shape=(shape(height + 1, 32, 128), shape(H...  6.24 us
    ppermute x1, starting transfers between devices, body(): east = lax.ppermute(near, 'gx', ring(across, -1))  5.32 us
    pallas_call x1, Pallas kernels, second_pass(): pl.pallas_call(second_kernel, out_shape=(jax.ShapeDtypeStruct((6, height,...  5.17 us
    pallas_call x1, Pallas kernels, pack(): pl.pallas_call(pack_kernel, out_shape=(jax.ShapeDtypeStruct((devices * SL...  4.84 us
    ppermute x1, starting transfers between devices, body(): down = lax.ppermute(top, 'gy', ring(along, -1))  2.94 us
    pallas_call x1, Pallas kernels, first_pass(): pl.pallas_call(first_kernel, out_shape=(jax.ShapeDtypeStruct((height + 2,...  2.57 us
  transfers between devices with their start and end apart: 5, of which 2 were waited for; matrix products, arithmetic and copies ran while one was open for 0% of the time, Pallas kernels for 5%

profile of v3, /device:TPU:0, one launch (start us, length us, event | category | flops | bytes accessed | tf_op | source)
XLA Modules:
  0.0 86.7 jit_solution(16254238798099730209)
XLA Ops:
  1.3 4.8 %pack.1 = (bf16[1664,8,128]{2,1,0:T(8,128)(2,1)}, f32[8,128]{1,0:T(8,128)}) custom-call(s32[1]{0:T(128)S(6)} %copy.10.count_ref, s32[1,1024]{1,0:T(1,128)} %bitcast.12, s32[1,1024]{1,0:T(1,128)} %bitcast.13, bf16[6,1024,128]{2,1,0:T(8,128)(2,1)} %bitcast.11, bf16[1024,128]{1,0:T(8,128)(2,1)} %weight_ref.1, s32[1024,128]{1,0:T(8,128)} %cols_ref.1), custom_call_target="tpu_custom_call" | custom-call | tf_op jit(solution)/shard_map/pack/pallas_call | solution.py:135
  6.1 0.0 copy-start.4
  6.1 12.1 %all-to-all-start = ((bf16[128,13,8,128]{3,2,1,0:T(8,128)(2,1)}), bf16[128,13,8,128]{3,2,1,0:T(8,128)(2,1)S(1)}, u32[]{:S(2)}, u32[]{:S(2)}) async-start(bf16[128,13,8,128]{3,2,1,0:T(8,128)(2,1)} %bitcast.10), calls=%async_computation | async-start | bytes 6815744 | tf_op jit(solution)/shard_map/all_to_all | solution.py:614
  18.2 0.1 add_convert_fusion.flags_ref
  18.3 0.0 copy-done.4
  18.3 0.0 copy-start
  18.3 1.0 %copy-done = f32[256,256]{1,0:T(8,128)S(1)} copy-done((f32[256,256]{1,0:T(8,128)S(1)}, f32[256,256]{1,0:T(8,128)}, u32[]{:S(2)}) %copy-start) | copy-done | bytes 262168
  19.3 0.0 copy-start.2
  19.3 0.9 %copy-done.2 = f32[256,256]{1,0:T(8,128)S(1)} copy-done((f32[256,256]{1,0:T(8,128)S(1)}, f32[256,256]{1,0:T(8,128)}, u32[]{:S(2)}) %copy-start.2) | copy-done | bytes 262168
  20.2 0.7 coefficient_edges.1
  21.0 41.8 %all-to-all-done = bf16[128,13,8,128]{3,2,1,0:T(8,128)(2,1)S(1)} async-done(((bf16[128,13,8,128]{3,2,1,0:T(8,128)(2,1)}), bf16[128,13,8,128]{3,2,1,0:T(8,128)(2,1)S(1)}, u32[]{:S(2)}, u32[]{:S(2)}) %all-to-all-start) | async-done | bytes 3407904 | tf_op jit(solution)/shard_map/all_to_all | solution.py:614
  62.8 0.0 copy-start.1
  62.8 0.0 copy-start.3
  62.8 6.2 %bin.1 = (f32[257,32,128]{2,1,0:T(8,128)S(1)}, f32[3,8,256]{2,1,0:T(8,128)S(1)}, f32[3,8,256]{2,1,0:T(8,128)S(1)}) custom-call(bf16[1664,8,128]{2,1,0:T(8,128)(2,1)S(1)} %bitcast.9, f32[8,256]{1,0:T(8,128)S(1)} %get-tuple-element.17.edge_top, f32[8,256]{1,0:T(8,128)S(1)} %get-tuple-element.18.edge_bottom), custom_call_target="tpu_custom_call" | custom-call | tf_op jit(solution)/shard_map/bin/pallas_call | solution.py:291
  69.0 0.0 collective-permute-start
  69.1 2.9 %collective-permute-start.1 = (f32[3,8,256]{2,1,0:T(8,128)S(1)}, f32[3,8,256]{2,1,0:T(8,128)S(1)}, u32[]{:S(2)}, u32[]{:S(2)}) collective-permute-start(f32[3,8,256]{2,1,0:T(8,128)S(1)} %get-tuple-element.21), channel_id=1, source_target_pairs={{0,7},{1,0},{2,1},{3,2},{4,3},{5,4},{6,5},{7,6},{8,15},{9,8},{10,9... | collective-permute-start | bytes 73736 | tf_op jit(solution)/shard_map/ppermute | solution.py:626
  72.0 1.1 %column_strips.1 = (f32[5,8,128]{2,1,0:T(8,128)S(1)}, f32[5,8,128]{2,1,0:T(8,128)S(1)}) custom-call(f32[257,32,128]{2,1,0:T(8,128)S(1)} %get-tuple-element.19.acc_ref, f32[8,128]{1,0:T(8,128)S(1)} %get-tuple-element.24.edge_left, f32[8,128]{1,0:T(8,128)S(1)} %get-tuple-element.25.edge_right), custom_call_target="tpu_custom_call" | custom-call | tf_op jit(solution)/shard_map/column_strips/pallas_call | solution.py:336
  73.1 0.4 collective-permute-done.up_ref
  73.5 0.0 collective-permute-done.1.down_ref
  73.5 0.1 collective-permute-start.2
  73.6 5.3 %collective-permute-start.3 = (f32[7,8,128]{2,1,0:T(8,128)S(1)}, f32[7,8,128]{2,1,0:T(8,128)S(1)}, u32[]{:S(2)}, u32[]{:S(2)}) collective-permute-start(f32[7,8,128]{2,1,0:T(8,128)S(1)} %pad_maximum_fusion.1), channel_id=1, source_target_pairs={{0,120},{8,0},{16,8},{24,16},{32,24},{40,32},{48,40},{56,48},{64,5... | collective-permute-start | bytes 86024 | tf_op jit(solution)/shard_map/ppermute | solution.py:630
  78.9 0.0 copy-done.1
  78.9 0.0 copy-done.3
  78.9 2.6 %first_pass.1 = (f32[258,8,256]{2,1,0:T(8,128)S(1)}, f32[256,8,128]{2,1,0:T(8,128)S(1)}) custom-call(s32[4]{0:T(128)S(1)} %add_convert_fusion.flags_ref, f32[257,32,128]{2,1,0:T(8,128)S(1)} %get-tuple-element.19.acc_ref, f32[3,8,256]{2,1,0:T(8,128)S(1)} %collective-permute-done.up_ref, f32[3,8,256]{2,1,0:T(8,128)S(1)} %collective-permute-done.1.down_ref, ...), custom_call_target="tpu_custom_call" | custom-call | tf_op jit(solution)/shard_map/first_pass/pallas_call | solution.py:426
  81.5 0.0 collective-permute-done.2.west_ref
  81.5 0.0 collective-permute-done.3.east_ref
  81.5 5.2 %second_pass.1 = (f32[6,256,256]{2,1,0:T(8,128)}, f32[256,256]{1,0:T(8,128)}) custom-call(s32[4]{0:T(128)S(1)} %add_convert_fusion.flags_ref, f32[258,8,256]{2,1,0:T(8,128)S(1)} %get-tuple-element.22.once_ref, f32[256,8,128]{2,1,0:T(8,128)S(1)} %get-tuple-element.23.inner_ref, f32[3,8,256]{2,1,0:T(8,128)S(1)} %collective-permute-done.up_ref, ...), custom_call_target="tpu_custom_call" | custom-call | tf_op jit(solution)/shard_map/second_pass/pallas_call | solution.py:546
  (4 shorter events, 0.0 us)
Async XLA Ops:
  6.1 12.2 %copy-start.4 = (f32[8,128]{1,0:T(8,128)S(1)}, f32[8,128]{1,0:T(8,128)}, u32[]{:S(2)}) copy-start(f32[8,128]{1,0:T(8,128)} %get-tuple-element.16.after_ref) | copy-start | bytes 12292
  6.1 56.6 %all-to-all-start = ((bf16[128,13,8,128]{3,2,1,0:T(8,128)(2,1)}), bf16[128,13,8,128]{3,2,1,0:T(8,128)(2,1)S(1)}, u32[]{:S(2)}, u32[]{:S(2)}) async-start(bf16[128,13,8,128]{3,2,1,0:T(8,128)(2,1)} %bitcast.10), calls=%async_computation | async-start | bytes 6815744 | tf_op jit(solution)/shard_map/all_to_all | solution.py:614
  18.3 1.0 %copy-start = (f32[256,256]{1,0:T(8,128)S(1)}, f32[256,256]{1,0:T(8,128)}, u32[]{:S(2)}) copy-start(f32[256,256]{1,0:T(8,128)} %cx_ref.5) | copy-start | bytes 786436
  19.3 0.9 %copy-start.2 = (f32[256,256]{1,0:T(8,128)S(1)}, f32[256,256]{1,0:T(8,128)}, u32[]{:S(2)}) copy-start(f32[256,256]{1,0:T(8,128)} %cy_ref.5) | copy-start | bytes 786436
  62.8 16.2 %copy-start.1 = (f32[256,256]{1,0:T(8,128)S(1)}, f32[256,256]{1,0:T(8,128)}, u32[]{:S(2)}) copy-start(f32[256,256]{1,0:T(8,128)} %cx_ref.5) | copy-start | bytes 786436
  62.8 16.2 %copy-start.3 = (f32[256,256]{1,0:T(8,128)S(1)}, f32[256,256]{1,0:T(8,128)}, u32[]{:S(2)}) copy-start(f32[256,256]{1,0:T(8,128)} %cy_ref.5) | copy-start | bytes 786436
  69.0 4.5 %collective-permute-start = (f32[3,8,256]{2,1,0:T(8,128)S(1)}, f32[3,8,256]{2,1,0:T(8,128)S(1)}, u32[]{:S(2)}, u32[]{:S(2)}) collective-permute-start(f32[3,8,256]{2,1,0:T(8,128)S(1)} %get-tuple-element.20), channel_id=1, source_target_pairs={{0,1},{1,2},{2,3},{3,4},{4,5},{5,6},{6,7},{7,0},{8,9},{9,10},{10,1... | collective-permute-start | bytes 73736 | tf_op jit(solution)/shard_map/ppermute | solution.py:625
  69.1 4.5 %collective-permute-start.1 = (f32[3,8,256]{2,1,0:T(8,128)S(1)}, f32[3,8,256]{2,1,0:T(8,128)S(1)}, u32[]{:S(2)}, u32[]{:S(2)}) collective-permute-start(f32[3,8,256]{2,1,0:T(8,128)S(1)} %get-tuple-element.21), channel_id=1, source_target_pairs={{0,7},{1,0},{2,1},{3,2},{4,3},{5,4},{6,5},{7,6},{8,15},{9,8},{10,9... | collective-permute-start | bytes 73736 | tf_op jit(solution)/shard_map/ppermute | solution.py:626
  73.5 8.0 %collective-permute-start.2 = (f32[7,8,128]{2,1,0:T(8,128)S(1)}, f32[7,8,128]{2,1,0:T(8,128)S(1)}, u32[]{:S(2)}, u32[]{:S(2)}) collective-permute-start(f32[7,8,128]{2,1,0:T(8,128)S(1)} %pad_maximum_fusion), channel_id=1, source_target_pairs={{0,8},{8,16},{16,24},{24,32},{32,40},{40,48},{48,56},{56,64},{64,7... | collective-permute-start | bytes 86024 | tf_op jit(solution)/shard_map/ppermute | solution.py:629
  73.6 7.9 %collective-permute-start.3 = (f32[7,8,128]{2,1,0:T(8,128)S(1)}, f32[7,8,128]{2,1,0:T(8,128)S(1)}, u32[]{:S(2)}, u32[]{:S(2)}) collective-permute-start(f32[7,8,128]{2,1,0:T(8,128)S(1)} %pad_maximum_fusion.1), channel_id=1, source_target_pairs={{0,120},{8,0},{16,8},{24,16},{32,24},{40,32},{48,40},{56,48},{64,5... | collective-permute-start | bytes 86024 | tf_op jit(solution)/shard_map/ppermute | solution.py:630

commit v4 on v3

--- a/solution.py
+++ b/solution.py
@@ -12,7 +12,7 @@
 COUNT_LANE = 14
 CODES = 16
 ENTRIES = 896
-GROUP = 64
+GROUP = 96
 FIRST_ROWS = 64
 ROWS = 32
 FLOOR = 0.15
@@ -446,6 +446,8 @@
     east_ref,
     cx_ref,
     cy_ref,
+    gridded_out,
+    coverage_out,
     gridded_ref,
     coverage_ref,
     mix_near,
@@ -455,6 +457,7 @@
     twice,
     side_x,
     side_y,
+    sems,
 ):
     height, width = cx_ref.shape
     has_up, has_down = flags_ref[0] > 0, flags_ref[1] > 0
@@ -500,6 +503,17 @@
             first + jnp.where(lane == 0, along_x[0] * beside, 0.0),
             last + jnp.where(lane == 127, along_x[1] * beside, 0.0),
         ]
+
+    def write_out(block):
+        rows = pl.ds(pl.multiple_of(block * ROWS, ROWS), ROWS)
+        return (
+            pltpu.make_async_copy(
+                gridded_ref.at[:, rows, :], gridded_out.at[:, rows, :], sems.at[block, 0]
+            ),
+            pltpu.make_async_copy(
+                coverage_ref.at[rows, :], coverage_out.at[rows, :], sems.at[block, 1]
+            ),
+        )
 
     @pl.loop(0, steps + 1)
     def _(g):
@@ -539,6 +553,15 @@
             for half in range(2):
                 twice[half, pl.ds(pl.multiple_of((start + i) * 8, 8), 8), :] = fresh[half]
 
+        @pl.when(g > 0)
+        def _():
+            for copy in write_out(g - 1):
+                copy.start()
+
+    for block in range(steps):
+        for copy in write_out(block):
+            copy.wait()
+
 
 def second_pass(flags, once, inner, up, down, west, east, cx, cy):
     height, width = cx.shape
@@ -550,8 +573,10 @@
             jax.ShapeDtypeStruct((height, width), f32),
         ),
         in_specs=[pl.BlockSpec(memory_space=pltpu.SMEM)] + [vmem] * 8,
-        out_specs=(vmem, vmem),
+        out_specs=(pl.BlockSpec(memory_space=pltpu.HBM),) * 2,
         scratch_shapes=[
+            pltpu.VMEM((6, height, width), f32),
+            pltpu.VMEM((height, width), f32),
             pltpu.VMEM((4, 8, 128), f32),
             pltpu.VMEM((4, 8, 128), f32),
             pltpu.VMEM((height + 2, 8, 128), f32),
@@ -559,6 +584,7 @@
             pltpu.VMEM((width // 128, height * 8, 128), f32),
             pltpu.VMEM((height, 128), f32),
             pltpu.VMEM((height, 128), f32),
+            pltpu.SemaphoreType.DMA((height // ROWS, 2)),
         ],
         compiler_params=pltpu.CompilerParams(vmem_limit_bytes=24 << 20),
         name="second_pass",

time: 88.2 us -> 88.3 us (level); the launches traced: 86.7 us -> 88 us
  Pallas kernels: 20.6 us -> 21.8 us
    pallas_call x1, Pallas kernels: 6.24 us -> 7.84 us  [bin_blocks(): pl.pallas_call(bin_kernel, out_shape=(shape(height + 1, 32, 128), shape(H...]
where the time goes in v4:
time: 88.3 us; the launch traced here: 88 us
  waiting for transfers between devices  42.2 us (48%)
  Pallas kernels  21.8 us (25%)
  starting transfers between devices  20.5 us (23%)
  local copies, waits for them, and re-layouts  1.92 us (2%)
  between operations  1.39 us (2%)
    all_to_all x1, waiting for transfers between devices, body(): lax.all_to_all(message.reshape(devices, SLOTS, 8, 128), ('gx', 'gy'), spl...  41.8 us
    all_to_all x1, starting transfers between devices, body(): lax.all_to_all(message.reshape(devices, SLOTS, 8, 128), ('gx', 'gy'), spl...  12.1 us
    pallas_call x1, Pallas kernels, bin_blocks(): pl.pallas_call(bin_kernel, out_shape=(shape(height + 1, 32, 128), shape(H...  7.84 us
    ppermute x1, starting transfers between devices, body(): east = lax.ppermute(near, 'gx', ring(across, -1))  5.32 us
    pallas_call x1, Pallas kernels, second_pass(): pl.pallas_call(second_kernel, out_shape=(jax.ShapeDtypeStruct((6, height,...  4.82 us
    pallas_call x1, Pallas kernels, pack(): pl.pallas_call(pack_kernel, out_shape=(jax.ShapeDtypeStruct((devices * SL...  4.79 us
    ppermute x1, starting transfers between devices, body(): down = lax.ppermute(top, 'gy', ring(along, -1))  2.94 us
    pallas_call x1, Pallas kernels, first_pass(): pl.pallas_call(first_kernel, out_shape=(jax.ShapeDtypeStruct((height + 2,...  2.57 us
  transfers between devices with their start and end apart: 5, of which 2 were waited for; matrix products, arithmetic and copies ran while one was open for 0% of the time, Pallas kernels for 5%

profile of v4, /device:TPU:0, one launch (start us, length us, event | category | flops | bytes accessed | tf_op | source)
XLA Modules:
  0.0 88.0 jit_solution(16175054490801262351)
XLA Ops:
  1.3 4.8 %pack.1 = (bf16[1664,8,128]{2,1,0:T(8,128)(2,1)}, f32[8,128]{1,0:T(8,128)}) custom-call(s32[1]{0:T(128)S(6)} %copy.10.count_ref, s32[1,1024]{1,0:T(1,128)} %bitcast.12, s32[1,1024]{1,0:T(1,128)} %bitcast.13, bf16[6,1024,128]{2,1,0:T(8,128)(2,1)} %bitcast.11, bf16[1024,128]{1,0:T(8,128)(2,1)} %weight_ref.1, s32[1024,128]{1,0:T(8,128)} %cols_ref.1), custom_call_target="tpu_custom_call" | custom-call | tf_op jit(solution)/shard_map/pack/pallas_call | solution.py:135
  6.1 0.0 copy-start.4
  6.1 12.1 %all-to-all-start = ((bf16[128,13,8,128]{3,2,1,0:T(8,128)(2,1)}), bf16[128,13,8,128]{3,2,1,0:T(8,128)(2,1)S(1)}, u32[]{:S(2)}, u32[]{:S(2)}) async-start(bf16[128,13,8,128]{3,2,1,0:T(8,128)(2,1)} %bitcast.10), calls=%async_computation | async-start | bytes 6815744 | tf_op jit(solution)/shard_map/all_to_all | solution.py:640
  18.2 0.1 add_convert_fusion.flags_ref
  18.3 0.0 copy-done.4
  18.3 0.0 copy-start
  18.3 1.0 %copy-done = f32[256,256]{1,0:T(8,128)S(1)} copy-done((f32[256,256]{1,0:T(8,128)S(1)}, f32[256,256]{1,0:T(8,128)}, u32[]{:S(2)}) %copy-start) | copy-done | bytes 262168
  19.3 0.0 copy-start.2
  19.3 0.9 %copy-done.2 = f32[256,256]{1,0:T(8,128)S(1)} copy-done((f32[256,256]{1,0:T(8,128)S(1)}, f32[256,256]{1,0:T(8,128)}, u32[]{:S(2)}) %copy-start.2) | copy-done | bytes 262168
  20.2 0.7 coefficient_edges.1
  21.0 41.8 %all-to-all-done = bf16[128,13,8,128]{3,2,1,0:T(8,128)(2,1)S(1)} async-done(((bf16[128,13,8,128]{3,2,1,0:T(8,128)(2,1)}), bf16[128,13,8,128]{3,2,1,0:T(8,128)(2,1)S(1)}, u32[]{:S(2)}, u32[]{:S(2)}) %all-to-all-start) | async-done | bytes 3407904 | tf_op jit(solution)/shard_map/all_to_all | solution.py:640
  62.8 0.0 copy-start.1
  62.8 0.0 copy-start.3
  62.8 7.8 %bin.1 = (f32[257,32,128]{2,1,0:T(8,128)S(1)}, f32[3,8,256]{2,1,0:T(8,128)S(1)}, f32[3,8,256]{2,1,0:T(8,128)S(1)}) custom-call(bf16[1664,8,128]{2,1,0:T(8,128)(2,1)S(1)} %bitcast.9, f32[8,256]{1,0:T(8,128)S(1)} %get-tuple-element.17.edge_top, f32[8,256]{1,0:T(8,128)S(1)} %get-tuple-element.18.edge_bottom), custom_call_target="tpu_custom_call" | custom-call | tf_op jit(solution)/shard_map/bin/pallas_call | solution.py:291
  70.6 0.0 collective-permute-start
  70.7 2.9 %collective-permute-start.1 = (f32[3,8,256]{2,1,0:T(8,128)S(1)}, f32[3,8,256]{2,1,0:T(8,128)S(1)}, u32[]{:S(2)}, u32[]{:S(2)}) collective-permute-start(f32[3,8,256]{2,1,0:T(8,128)S(1)} %get-tuple-element.21), channel_id=1, source_target_pairs={{0,7},{1,0},{2,1},{3,2},{4,3},{5,4},{6,5},{7,6},{8,15},{9,8},{10,9... | collective-permute-start | bytes 73736 | tf_op jit(solution)/shard_map/ppermute | solution.py:652
  73.6 1.1 %column_strips.1 = (f32[5,8,128]{2,1,0:T(8,128)S(1)}, f32[5,8,128]{2,1,0:T(8,128)S(1)}) custom-call(f32[257,32,128]{2,1,0:T(8,128)S(1)} %get-tuple-element.19.acc_ref, f32[8,128]{1,0:T(8,128)S(1)} %get-tuple-element.24.edge_left, f32[8,128]{1,0:T(8,128)S(1)} %get-tuple-element.25.edge_right), custom_call_target="tpu_custom_call" | custom-call | tf_op jit(solution)/shard_map/column_strips/pallas_call | solution.py:336
  74.7 0.4 collective-permute-done.up_ref
  75.1 0.0 collective-permute-done.1.down_ref
  75.1 0.1 collective-permute-start.2
  75.2 5.3 %collective-permute-start.3 = (f32[7,8,128]{2,1,0:T(8,128)S(1)}, f32[7,8,128]{2,1,0:T(8,128)S(1)}, u32[]{:S(2)}, u32[]{:S(2)}) collective-permute-start(f32[7,8,128]{2,1,0:T(8,128)S(1)} %pad_maximum_fusion.1), channel_id=1, source_target_pairs={{0,120},{8,0},{16,8},{24,16},{32,24},{40,32},{48,40},{56,48},{64,5... | collective-permute-start | bytes 86024 | tf_op jit(solution)/shard_map/ppermute | solution.py:656
  80.5 0.0 copy-done.1
  80.5 0.0 copy-done.3
  80.5 2.6 %first_pass.1 = (f32[258,8,256]{2,1,0:T(8,128)S(1)}, f32[256,8,128]{2,1,0:T(8,128)S(1)}) custom-call(s32[4]{0:T(128)S(1)} %add_convert_fusion.flags_ref, f32[257,32,128]{2,1,0:T(8,128)S(1)} %get-tuple-element.19.acc_ref, f32[3,8,256]{2,1,0:T(8,128)S(1)} %collective-permute-done.up_ref, f32[3,8,256]{2,1,0:T(8,128)S(1)} %collective-permute-done.1.down_ref, ...), custom_call_target="tpu_custom_call" | custom-call | tf_op jit(solution)/shard_map/first_pass/pallas_call | solution.py:426
  83.1 0.0 collective-permute-done.2.west_ref
  83.1 0.0 collective-permute-done.3.east_ref
  83.1 4.8 %second_pass.1 = (f32[6,256,256]{2,1,0:T(8,128)}, f32[256,256]{1,0:T(8,128)}) custom-call(s32[4]{0:T(128)S(1)} %add_convert_fusion.flags_ref, f32[258,8,256]{2,1,0:T(8,128)S(1)} %get-tuple-element.22.once_ref, f32[256,8,128]{2,1,0:T(8,128)S(1)} %get-tuple-element.23.inner_ref, f32[3,8,256]{2,1,0:T(8,128)S(1)} %collective-permute-done.up_ref, ...), custom_call_target="tpu_custom_call" | custom-call | tf_op jit(solution)/shard_map/second_pass/pallas_call | solution.py:569
  (4 shorter events, 0.0 us)
Async XLA Ops:
  6.1 12.2 %copy-start.4 = (f32[8,128]{1,0:T(8,128)S(1)}, f32[8,128]{1,0:T(8,128)}, u32[]{:S(2)}) copy-start(f32[8,128]{1,0:T(8,128)} %get-tuple-element.16.after_ref) | copy-start | bytes 12292
  6.1 56.7 %all-to-all-start = ((bf16[128,13,8,128]{3,2,1,0:T(8,128)(2,1)}), bf16[128,13,8,128]{3,2,1,0:T(8,128)(2,1)S(1)}, u32[]{:S(2)}, u32[]{:S(2)}) async-start(bf16[128,13,8,128]{3,2,1,0:T(8,128)(2,1)} %bitcast.10), calls=%async_computation | async-start | bytes 6815744 | tf_op jit(solution)/shard_map/all_to_all | solution.py:640
  18.3 1.0 %copy-start = (f32[256,256]{1,0:T(8,128)S(1)}, f32[256,256]{1,0:T(8,128)}, u32[]{:S(2)}) copy-start(f32[256,256]{1,0:T(8,128)} %cx_ref.5) | copy-start | bytes 786436
  19.3 0.9 %copy-start.2 = (f32[256,256]{1,0:T(8,128)S(1)}, f32[256,256]{1,0:T(8,128)}, u32[]{:S(2)}) copy-start(f32[256,256]{1,0:T(8,128)} %cy_ref.5) | copy-start | bytes 786436
  62.8 17.8 %copy-start.1 = (f32[256,256]{1,0:T(8,128)S(1)}, f32[256,256]{1,0:T(8,128)}, u32[]{:S(2)}) copy-start(f32[256,256]{1,0:T(8,128)} %cx_ref.5) | copy-start | bytes 786436
  62.8 17.8 %copy-start.3 = (f32[256,256]{1,0:T(8,128)S(1)}, f32[256,256]{1,0:T(8,128)}, u32[]{:S(2)}) copy-start(f32[256,256]{1,0:T(8,128)} %cy_ref.5) | copy-start | bytes 786436
  70.6 4.5 %collective-permute-start = (f32[3,8,256]{2,1,0:T(8,128)S(1)}, f32[3,8,256]{2,1,0:T(8,128)S(1)}, u32[]{:S(2)}, u32[]{:S(2)}) collective-permute-start(f32[3,8,256]{2,1,0:T(8,128)S(1)} %get-tuple-element.20), channel_id=1, source_target_pairs={{0,1},{1,2},{2,3},{3,4},{4,5},{5,6},{6,7},{7,0},{8,9},{9,10},{10,1... | collective-permute-start | bytes 73736 | tf_op jit(solution)/shard_map/ppermute | solution.py:651
  70.7 4.5 %collective-permute-start.1 = (f32[3,8,256]{2,1,0:T(8,128)S(1)}, f32[3,8,256]{2,1,0:T(8,128)S(1)}, u32[]{:S(2)}, u32[]{:S(2)}) collective-permute-start(f32[3,8,256]{2,1,0:T(8,128)S(1)} %get-tuple-element.21), channel_id=1, source_target_pairs={{0,7},{1,0},{2,1},{3,2},{4,3},{5,4},{6,5},{7,6},{8,15},{9,8},{10,9... | collective-permute-start | bytes 73736 | tf_op jit(solution)/shard_map/ppermute | solution.py:652
  75.1 8.0 %collective-permute-start.2 = (f32[7,8,128]{2,1,0:T(8,128)S(1)}, f32[7,8,128]{2,1,0:T(8,128)S(1)}, u32[]{:S(2)}, u32[]{:S(2)}) collective-permute-start(f32[7,8,128]{2,1,0:T(8,128)S(1)} %pad_maximum_fusion), channel_id=1, source_target_pairs={{0,8},{8,16},{16,24},{24,32},{32,40},{40,48},{48,56},{56,64},{64,7... | collective-permute-start | bytes 86024 | tf_op jit(solution)/shard_map/ppermute | solution.py:655
  75.2 7.9 %collective-permute-start.3 = (f32[7,8,128]{2,1,0:T(8,128)S(1)}, f32[7,8,128]{2,1,0:T(8,128)S(1)}, u32[]{:S(2)}, u32[]{:S(2)}) collective-permute-start(f32[7,8,128]{2,1,0:T(8,128)S(1)} %pad_maximum_fusion.1), channel_id=1, source_target_pairs={{0,120},{8,0},{16,8},{24,16},{32,24},{40,32},{48,40},{56,48},{64,5... | collective-permute-start | bytes 86024 | tf_op jit(solution)/shard_map/ppermute | solution.py:656

commit v5 on v4

--- a/solution.py
+++ b/solution.py
@@ -106,7 +106,7 @@
     for load in loads[2:]:
         load.wait()
 
-    @pl.loop(0, blocks // 16, unroll=4)
+    @pl.loop(0, blocks // 16, unroll=8)
     def _(g):
         near = pl.ds(pl.multiple_of(g * 16, 16), 16)
         weight = weight_v[near, :].astype(f32)
@@ -117,13 +117,13 @@
 
     copy.wait()
 
-    @pl.loop(0, (live_count + 15) // 16)
+    @pl.loop(0, (live_count + 31) // 32)
     def _(group):
-        for i in range(16):
-            b = group * 16 + i
+        for i in range(32):
+            b = group * 32 + i
             out_ref[slot_s[0, b]] = rows_f[pl.ds(pl.multiple_of(b * 8, 8), 8), :].astype(bf16)
 
-    @pl.loop(0, devices, unroll=4)
+    @pl.loop(0, devices, unroll=16)
     def _(t):
         code = codes_f[pl.ds(t, 1), :]
         out_ref[t * SLOTS + CAPACITY] = jnp.broadcast_to(code, (8, 128)).astype(bf16)
@@ -174,10 +174,10 @@
     sources = msg_ref.shape[0] // SLOTS
     height = acc_ref.shape[0] - 1
 
-    @pl.loop(0, sources // 8)
+    @pl.loop(0, sources // 16)
     def _(g):
-        for i in range(8):
-            s = g * 8 + i
+        for i in range(16):
+            s = g * 16 + i
             tile = msg_ref[s * SLOTS + CAPACITY].astype(f32)
             codes_v[pl.ds(s, 1), :] = tile[0:1, :]
 
@@ -322,7 +322,7 @@
             result.append(jnp.where(here, last, carry[2 * q + 1]))
         return tuple(result)
 
-    strips = lax.fori_loop(0, 64, take, (blank,) * 8, unroll=8)
+    strips = lax.fori_loop(0, 64, take, (blank,) * 8, unroll=16)
     for q in range(4):
         left_ref[q] = strips[2 * q]
         right_ref[q] = strips[2 * q + 1]

time: 88.3 us -> 87.8 us (level)
  starting transfers between devices: 20.5 us -> 19.5 us
    ppermute x1, starting transfers between devices: 0.07 us -> 1.78 us  [body(): west = lax.ppermute(far, 'gx', ring(across, 1))]
    ppermute x1, starting transfers between devices: 5.32 us -> 3.63 us  [body(): east = lax.ppermute(near, 'gx', ring(across, -1))]
    all_to_all x1, starting transfers between devices: 12.1 us -> 11.1 us  [body(): lax.all_to_all(message.reshape(devices, SLOTS, 8, 128), ('gx', 'gy'), spl...]
where the time goes in v5:
time: 87.8 us; the launch traced here: 87.6 us
  waiting for transfers between devices  42.5 us (48%)
  Pallas kernels  22.2 us (25%)
  starting transfers between devices  19.5 us (22%)
  local copies, waits for them, and re-layouts  1.92 us (2%)
  between operations  1.38 us (2%)
    all_to_all x1, waiting for transfers between devices, body(): lax.all_to_all(message.reshape(devices, SLOTS, 8, 128), ('gx', 'gy'), spl...  41.8 us
    all_to_all x1, starting transfers between devices, body(): lax.all_to_all(message.reshape(devices, SLOTS, 8, 128), ('gx', 'gy'), spl...  11.1 us
    pallas_call x1, Pallas kernels, bin_blocks(): pl.pallas_call(bin_kernel, out_shape=(shape(height + 1, 32, 128), shape(H...  7.84 us
    pallas_call x1, Pallas kernels, pack(): pl.pallas_call(pack_kernel, out_shape=(jax.ShapeDtypeStruct((devices * SL...  5.43 us
    pallas_call x1, Pallas kernels, second_pass(): pl.pallas_call(second_kernel, out_shape=(jax.ShapeDtypeStruct((6, height,...  4.82 us
    ppermute x1, starting transfers between devices, body(): east = lax.ppermute(near, 'gx', ring(across, -1))  3.63 us
    ppermute x1, starting transfers between devices, body(): down = lax.ppermute(top, 'gy', ring(along, -1))  2.94 us
    pallas_call x1, Pallas kernels, first_pass(): pl.pallas_call(first_kernel, out_shape=(jax.ShapeDtypeStruct((height + 2,...  2.57 us
  transfers between devices with their start and end apart: 5, of which 2 were waited for; matrix products, arithmetic and copies ran while one was open for 0% of the time, Pallas kernels for 5%

profile of v5, /device:TPU:0, one launch (start us, length us, event | category | flops | bytes accessed | tf_op | source)
XLA Modules:
  0.0 87.6 jit_solution(9297194704994640837)
XLA Ops:
  1.3 5.4 %pack.1 = (bf16[1664,8,128]{2,1,0:T(8,128)(2,1)}, f32[8,128]{1,0:T(8,128)}) custom-call(s32[1]{0:T(128)S(6)} %copy.10.count_ref, s32[1,1024]{1,0:T(1,128)} %bitcast.12, s32[1,1024]{1,0:T(1,128)} %bitcast.13, bf16[6,1024,128]{2,1,0:T(8,128)(2,1)} %bitcast.11, bf16[1024,128]{1,0:T(8,128)(2,1)} %weight_ref.1, s32[1024,128]{1,0:T(8,128)} %cols_ref.1), custom_call_target="tpu_custom_call" | custom-call | tf_op jit(solution)/shard_map/pack/pallas_call | solution.py:135
  6.7 0.0 copy-start.4
  6.7 11.1 %all-to-all-start = ((bf16[128,13,8,128]{3,2,1,0:T(8,128)(2,1)}), bf16[128,13,8,128]{3,2,1,0:T(8,128)(2,1)S(1)}, u32[]{:S(2)}, u32[]{:S(2)}) async-start(bf16[128,13,8,128]{3,2,1,0:T(8,128)(2,1)} %bitcast.10), calls=%async_computation | async-start | bytes 6815744 | tf_op jit(solution)/shard_map/all_to_all | solution.py:640
  17.9 0.1 add_convert_fusion.flags_ref
  18.0 0.0 copy-done.4
  18.0 0.0 copy-start
  18.0 1.0 %copy-done = f32[256,256]{1,0:T(8,128)S(1)} copy-done((f32[256,256]{1,0:T(8,128)S(1)}, f32[256,256]{1,0:T(8,128)}, u32[]{:S(2)}) %copy-start) | copy-done | bytes 262168
  18.9 0.0 copy-start.2
  18.9 0.9 %copy-done.2 = f32[256,256]{1,0:T(8,128)S(1)} copy-done((f32[256,256]{1,0:T(8,128)S(1)}, f32[256,256]{1,0:T(8,128)}, u32[]{:S(2)}) %copy-start.2) | copy-done | bytes 262168
  19.9 0.7 coefficient_edges.1
  20.6 41.8 %all-to-all-done = bf16[128,13,8,128]{3,2,1,0:T(8,128)(2,1)S(1)} async-done(((bf16[128,13,8,128]{3,2,1,0:T(8,128)(2,1)}), bf16[128,13,8,128]{3,2,1,0:T(8,128)(2,1)S(1)}, u32[]{:S(2)}, u32[]{:S(2)}) %all-to-all-start) | async-done | bytes 3407904 | tf_op jit(solution)/shard_map/all_to_all | solution.py:640
  62.4 0.0 copy-start.1
  62.4 0.0 copy-start.3
  62.4 7.8 %bin.1 = (f32[257,32,128]{2,1,0:T(8,128)S(1)}, f32[3,8,256]{2,1,0:T(8,128)S(1)}, f32[3,8,256]{2,1,0:T(8,128)S(1)}) custom-call(bf16[1664,8,128]{2,1,0:T(8,128)(2,1)S(1)} %bitcast.9, f32[8,256]{1,0:T(8,128)S(1)} %get-tuple-element.17.edge_top, f32[8,256]{1,0:T(8,128)S(1)} %get-tuple-element.18.edge_bottom), custom_call_target="tpu_custom_call" | custom-call | tf_op jit(solution)/shard_map/bin/pallas_call | solution.py:291
  70.3 0.0 collective-permute-start
  70.3 2.9 %collective-permute-start.1 = (f32[3,8,256]{2,1,0:T(8,128)S(1)}, f32[3,8,256]{2,1,0:T(8,128)S(1)}, u32[]{:S(2)}, u32[]{:S(2)}) collective-permute-start(f32[3,8,256]{2,1,0:T(8,128)S(1)} %get-tuple-element.21), channel_id=1, source_target_pairs={{0,7},{1,0},{2,1},{3,2},{4,3},{5,4},{6,5},{7,6},{8,15},{9,8},{10,9... | collective-permute-start | bytes 73736 | tf_op jit(solution)/shard_map/ppermute | solution.py:652
  73.3 0.8 column_strips.1
  74.1 0.7 collective-permute-done.up_ref
  74.8 0.0 collective-permute-done.1.down_ref
  74.8 1.8 %collective-permute-start.2 = (f32[7,8,128]{2,1,0:T(8,128)S(1)}, f32[7,8,128]{2,1,0:T(8,128)S(1)}, u32[]{:S(2)}, u32[]{:S(2)}) collective-permute-start(f32[7,8,128]{2,1,0:T(8,128)S(1)} %pad_maximum_fusion), channel_id=1, source_target_pairs={{0,8},{8,16},{16,24},{24,32},{32,40},{40,48},{48,56},{56,64},{64,7... | collective-permute-start | bytes 86024 | tf_op jit(solution)/shard_map/ppermute | solution.py:655
  76.6 3.6 %collective-permute-start.3 = (f32[7,8,128]{2,1,0:T(8,128)S(1)}, f32[7,8,128]{2,1,0:T(8,128)S(1)}, u32[]{:S(2)}, u32[]{:S(2)}) collective-permute-start(f32[7,8,128]{2,1,0:T(8,128)S(1)} %pad_maximum_fusion.1), channel_id=1, source_target_pairs={{0,120},{8,0},{16,8},{24,16},{32,24},{40,32},{48,40},{56,48},{64,5... | collective-permute-start | bytes 86024 | tf_op jit(solution)/shard_map/ppermute | solution.py:656
  80.2 0.0 copy-done.1
  80.2 0.0 copy-done.3
  80.2 2.6 %first_pass.1 = (f32[258,8,256]{2,1,0:T(8,128)S(1)}, f32[256,8,128]{2,1,0:T(8,128)S(1)}) custom-call(s32[4]{0:T(128)S(1)} %add_convert_fusion.flags_ref, f32[257,32,128]{2,1,0:T(8,128)S(1)} %get-tuple-element.19.acc_ref, f32[3,8,256]{2,1,0:T(8,128)S(1)} %collective-permute-done.up_ref, f32[3,8,256]{2,1,0:T(8,128)S(1)} %collective-permute-done.1.down_ref, ...), custom_call_target="tpu_custom_call" | custom-call | tf_op jit(solution)/shard_map/first_pass/pallas_call | solution.py:426
  82.8 0.0 collective-permute-done.2.west_ref
  82.8 0.0 collective-permute-done.3.east_ref
  82.8 4.8 %second_pass.1 = (f32[6,256,256]{2,1,0:T(8,128)}, f32[256,256]{1,0:T(8,128)}) custom-call(s32[4]{0:T(128)S(1)} %add_convert_fusion.flags_ref, f32[258,8,256]{2,1,0:T(8,128)S(1)} %get-tuple-element.22.once_ref, f32[256,8,128]{2,1,0:T(8,128)S(1)} %get-tuple-element.23.inner_ref, f32[3,8,256]{2,1,0:T(8,128)S(1)} %collective-permute-done.up_ref, ...), custom_call_target="tpu_custom_call" | custom-call | tf_op jit(solution)/shard_map/second_pass/pallas_call | solution.py:569
  (4 shorter events, 0.0 us)
Async XLA Ops:
  6.7 11.3 %copy-start.4 = (f32[8,128]{1,0:T(8,128)S(1)}, f32[8,128]{1,0:T(8,128)}, u32[]{:S(2)}) copy-start(f32[8,128]{1,0:T(8,128)} %get-tuple-element.16.after_ref) | copy-start | bytes 12292
  6.7 55.7 %all-to-all-start = ((bf16[128,13,8,128]{3,2,1,0:T(8,128)(2,1)}), bf16[128,13,8,128]{3,2,1,0:T(8,128)(2,1)S(1)}, u32[]{:S(2)}, u32[]{:S(2)}) async-start(bf16[128,13,8,128]{3,2,1,0:T(8,128)(2,1)} %bitcast.10), calls=%async_computation | async-start | bytes 6815744 | tf_op jit(solution)/shard_map/all_to_all | solution.py:640
  18.0 1.0 %copy-start = (f32[256,256]{1,0:T(8,128)S(1)}, f32[256,256]{1,0:T(8,128)}, u32[]{:S(2)}) copy-start(f32[256,256]{1,0:T(8,128)} %cx_ref.5) | copy-start | bytes 786436
  18.9 0.9 %copy-start.2 = (f32[256,256]{1,0:T(8,128)S(1)}, f32[256,256]{1,0:T(8,128)}, u32[]{:S(2)}) copy-start(f32[256,256]{1,0:T(8,128)} %cy_ref.5) | copy-start | bytes 786436
  62.4 17.8 %copy-start.1 = (f32[256,256]{1,0:T(8,128)S(1)}, f32[256,256]{1,0:T(8,128)}, u32[]{:S(2)}) copy-start(f32[256,256]{1,0:T(8,128)} %cx_ref.5) | copy-start | bytes 786436
  62.4 17.8 %copy-start.3 = (f32[256,256]{1,0:T(8,128)S(1)}, f32[256,256]{1,0:T(8,128)}, u32[]{:S(2)}) copy-start(f32[256,256]{1,0:T(8,128)} %cy_ref.5) | copy-start | bytes 786436
  70.3 4.5 %collective-permute-start = (f32[3,8,256]{2,1,0:T(8,128)S(1)}, f32[3,8,256]{2,1,0:T(8,128)S(1)}, u32[]{:S(2)}, u32[]{:S(2)}) collective-permute-start(f32[3,8,256]{2,1,0:T(8,128)S(1)} %get-tuple-element.20), channel_id=1, source_target_pairs={{0,1},{1,2},{2,3},{3,4},{4,5},{5,6},{6,7},{7,0},{8,9},{9,10},{10,1... | collective-permute-start | bytes 73736 | tf_op jit(solution)/shard_map/ppermute | solution.py:651
  70.3 4.5 %collective-permute-start.1 = (f32[3,8,256]{2,1,0:T(8,128)S(1)}, f32[3,8,256]{2,1,0:T(8,128)S(1)}, u32[]{:S(2)}, u32[]{:S(2)}) collective-permute-start(f32[3,8,256]{2,1,0:T(8,128)S(1)} %get-tuple-element.21), channel_id=1, source_target_pairs={{0,7},{1,0},{2,1},{3,2},{4,3},{5,4},{6,5},{7,6},{8,15},{9,8},{10,9... | collective-permute-start | bytes 73736 | tf_op jit(solution)/shard_map/ppermute | solution.py:652
  74.8 8.0 %collective-permute-start.2 = (f32[7,8,128]{2,1,0:T(8,128)S(1)}, f32[7,8,128]{2,1,0:T(8,128)S(1)}, u32[]{:S(2)}, u32[]{:S(2)}) collective-permute-start(f32[7,8,128]{2,1,0:T(8,128)S(1)} %pad_maximum_fusion), channel_id=1, source_target_pairs={{0,8},{8,16},{16,24},{24,32},{32,40},{40,48},{48,56},{56,64},{64,7... | collective-permute-start | bytes 86024 | tf_op jit(solution)/shard_map/ppermute | solution.py:655
  76.6 6.2 %collective-permute-start.3 = (f32[7,8,128]{2,1,0:T(8,128)S(1)}, f32[7,8,128]{2,1,0:T(8,128)S(1)}, u32[]{:S(2)}, u32[]{:S(2)}) collective-permute-start(f32[7,8,128]{2,1,0:T(8,128)S(1)} %pad_maximum_fusion.1), channel_id=1, source_target_pairs={{0,120},{8,0},{16,8},{24,16},{32,24},{40,32},{48,40},{56,48},{64,5... | collective-permute-start | bytes 86024 | tf_op jit(solution)/shard_map/ppermute | solution.py:656

commit v6 on v5

--- a/solution.py
+++ b/solution.py
@@ -471,7 +471,7 @@
         mix_near[q] = jnp.where(even, pltpu.roll(west, 127, 1), pltpu.roll(east, 127, 1))
         mix_far[q] = jnp.where(even, west, pltpu.roll(east, 126, 1))
 
-    @pl.loop(0, 64, unroll=16)
+    @pl.loop(0, 64, unroll=64)
     def _(j):
         for q in range(4):
             near[q * 64 + j + 1] = pltpu.roll(mix_near[q], 128 - 2 * j, 1)

time: 87.8 us -> 86.4 us (0.984); the launches traced: 87.6 us -> 85.1 us
  Pallas kernels: 22.2 us -> 19.9 us
    pallas_call x1, Pallas kernels: 7.84 us -> 5.87 us  [bin_blocks(): pl.pallas_call(bin_kernel, out_shape=(shape(height + 1, 32, 128), shape(H...]
    ppermute x1, starting transfers between devices: 0.02 us -> 1.33 us  [body(): up = lax.ppermute(bottom, 'gy', ring(along, 1))]
    ppermute x1, starting transfers between devices: 2.94 us -> 1.64 us  [body(): down = lax.ppermute(top, 'gy', ring(along, -1))]
    ppermute x1, starting transfers between devices: 3.63 us -> 4.65 us  [body(): east = lax.ppermute(near, 'gx', ring(across, -1))]
    ppermute x1, starting transfers between devices: 1.78 us -> 0.75 us  [body(): west = lax.ppermute(far, 'gx', ring(across, 1))]
where the time goes in v6:
time: 86.4 us; the launch traced here: 85.1 us
  waiting for transfers between devices  42.5 us (49%)
  Pallas kernels  19.9 us (23%)
  starting transfers between devices  19.3 us (22%)
  local copies, waits for them, and re-layouts  1.92 us (2%)
  between operations  1.37 us (2%)
    all_to_all x1, waiting for transfers between devices, body(): lax.all_to_all(message.reshape(devices, SLOTS, 8, 128), ('gx', 'gy'), spl...  41.8 us
    all_to_all x1, starting transfers between devices, body(): lax.all_to_all(message.reshape(devices, SLOTS, 8, 128), ('gx', 'gy'), spl...  10.9 us
    pallas_call x1, Pallas kernels, bin_blocks(): pl.pallas_call(bin_kernel, out_shape=(shape(height + 1, 32, 128), shape(H...  5.87 us
    pallas_call x1, Pallas kernels, pack(): pl.pallas_call(pack_kernel, out_shape=(jax.ShapeDtypeStruct((devices * SL...  5.43 us
    ppermute x1, starting transfers between devices, body(): east = lax.ppermute(near, 'gx', ring(across, -1))  4.65 us
    pallas_call x1, Pallas kernels, second_pass(): pl.pallas_call(second_kernel, out_shape=(jax.ShapeDtypeStruct((6, height,...  4.53 us
    pallas_call x1, Pallas kernels, first_pass(): pl.pallas_call(first_kernel, out_shape=(jax.ShapeDtypeStruct((height + 2,...  2.57 us
    unnamed x10, local copies, waits for them, and re-layouts  1.92 us
  transfers between devices with their start and end apart: 5, of which 2 were waited for; matrix products, arithmetic and copies ran while one was open for 0% of the time, Pallas kernels for 5%

profile of v6, /device:TPU:0, one launch (start us, length us, event | category | flops | bytes accessed | tf_op | source)
XLA Modules:
  0.0 85.1 jit_solution(11710387356414100640)
XLA Ops:
  1.3 5.4 %pack.1 = (bf16[1664,8,128]{2,1,0:T(8,128)(2,1)}, f32[8,128]{1,0:T(8,128)}) custom-call(s32[1]{0:T(128)S(6)} %copy.10.count_ref, s32[1,1024]{1,0:T(1,128)} %bitcast.12, s32[1,1024]{1,0:T(1,128)} %bitcast.13, bf16[6,1024,128]{2,1,0:T(8,128)(2,1)} %bitcast.11, bf16[1024,128]{1,0:T(8,128)(2,1)} %weight_ref.1, s32[1024,128]{1,0:T(8,128)} %cols_ref.1), custom_call_target="tpu_custom_call" | custom-call | tf_op jit(solution)/shard_map/pack/pallas_call | solution.py:135
  6.7 0.0 copy-start.4
  6.7 10.9 %all-to-all-start = ((bf16[128,13,8,128]{3,2,1,0:T(8,128)(2,1)}), bf16[128,13,8,128]{3,2,1,0:T(8,128)(2,1)S(1)}, u32[]{:S(2)}, u32[]{:S(2)}) async-start(bf16[128,13,8,128]{3,2,1,0:T(8,128)(2,1)} %bitcast.10), calls=%async_computation | async-start | bytes 6815744 | tf_op jit(solution)/shard_map/all_to_all | solution.py:640
  17.6 0.1 add_convert_fusion.flags_ref
  17.7 0.0 copy-done.4
  17.7 0.0 copy-start
  17.7 1.0 %copy-done = f32[256,256]{1,0:T(8,128)S(1)} copy-done((f32[256,256]{1,0:T(8,128)S(1)}, f32[256,256]{1,0:T(8,128)}, u32[]{:S(2)}) %copy-start) | copy-done | bytes 262168
  18.7 0.0 copy-start.2
  18.7 0.9 %copy-done.2 = f32[256,256]{1,0:T(8,128)S(1)} copy-done((f32[256,256]{1,0:T(8,128)S(1)}, f32[256,256]{1,0:T(8,128)}, u32[]{:S(2)}) %copy-start.2) | copy-done | bytes 262168
  19.6 0.7 coefficient_edges.1
  20.4 41.8 %all-to-all-done = bf16[128,13,8,128]{3,2,1,0:T(8,128)(2,1)S(1)} async-done(((bf16[128,13,8,128]{3,2,1,0:T(8,128)(2,1)}), bf16[128,13,8,128]{3,2,1,0:T(8,128)(2,1)S(1)}, u32[]{:S(2)}, u32[]{:S(2)}) %all-to-all-start) | async-done | bytes 3407904 | tf_op jit(solution)/shard_map/all_to_all | solution.py:640
  62.2 0.0 copy-start.1
  62.2 0.0 copy-start.3
  62.2 5.9 %bin.1 = (f32[257,32,128]{2,1,0:T(8,128)S(1)}, f32[3,8,256]{2,1,0:T(8,128)S(1)}, f32[3,8,256]{2,1,0:T(8,128)S(1)}) custom-call(bf16[1664,8,128]{2,1,0:T(8,128)(2,1)S(1)} %bitcast.9, f32[8,256]{1,0:T(8,128)S(1)} %get-tuple-element.17.edge_top, f32[8,256]{1,0:T(8,128)S(1)} %get-tuple-element.18.edge_bottom), custom_call_target="tpu_custom_call" | custom-call | tf_op jit(solution)/shard_map/bin/pallas_call | solution.py:291
  68.0 1.3 %collective-permute-start = (f32[3,8,256]{2,1,0:T(8,128)S(1)}, f32[3,8,256]{2,1,0:T(8,128)S(1)}, u32[]{:S(2)}, u32[]{:S(2)}) collective-permute-start(f32[3,8,256]{2,1,0:T(8,128)S(1)} %get-tuple-element.20), channel_id=1, source_target_pairs={{0,1},{1,2},{2,3},{3,4},{4,5},{5,6},{6,7},{7,0},{8,9},{9,10},{10,1... | collective-permute-start | bytes 73736 | tf_op jit(solution)/shard_map/ppermute | solution.py:651
  69.4 1.6 %collective-permute-start.1 = (f32[3,8,256]{2,1,0:T(8,128)S(1)}, f32[3,8,256]{2,1,0:T(8,128)S(1)}, u32[]{:S(2)}, u32[]{:S(2)}) collective-permute-start(f32[3,8,256]{2,1,0:T(8,128)S(1)} %get-tuple-element.21), channel_id=1, source_target_pairs={{0,7},{1,0},{2,1},{3,2},{4,3},{5,4},{6,5},{7,6},{8,15},{9,8},{10,9... | collective-permute-start | bytes 73736 | tf_op jit(solution)/shard_map/ppermute | solution.py:652
  71.0 0.8 column_strips.1
  71.8 0.7 collective-permute-done.up_ref
  72.5 0.0 collective-permute-done.1.down_ref
  72.5 0.8 collective-permute-start.2
  73.3 4.7 %collective-permute-start.3 = (f32[7,8,128]{2,1,0:T(8,128)S(1)}, f32[7,8,128]{2,1,0:T(8,128)S(1)}, u32[]{:S(2)}, u32[]{:S(2)}) collective-permute-start(f32[7,8,128]{2,1,0:T(8,128)S(1)} %pad_maximum_fusion.1), channel_id=1, source_target_pairs={{0,120},{8,0},{16,8},{24,16},{32,24},{40,32},{48,40},{56,48},{64,5... | collective-permute-start | bytes 86024 | tf_op jit(solution)/shard_map/ppermute | solution.py:656
  78.0 0.0 copy-done.1
  78.0 0.0 copy-done.3
  78.0 2.6 %first_pass.1 = (f32[258,8,256]{2,1,0:T(8,128)S(1)}, f32[256,8,128]{2,1,0:T(8,128)S(1)}) custom-call(s32[4]{0:T(128)S(1)} %add_convert_fusion.flags_ref, f32[257,32,128]{2,1,0:T(8,128)S(1)} %get-tuple-element.19.acc_ref, f32[3,8,256]{2,1,0:T(8,128)S(1)} %collective-permute-done.up_ref, f32[3,8,256]{2,1,0:T(8,128)S(1)} %collective-permute-done.1.down_ref, ...), custom_call_target="tpu_custom_call" | custom-call | tf_op jit(solution)/shard_map/first_pass/pallas_call | solution.py:426
  80.5 0.0 collective-permute-done.2.west_ref
  80.5 0.0 collective-permute-done.3.east_ref
  80.6 4.5 %second_pass.1 = (f32[6,256,256]{2,1,0:T(8,128)}, f32[256,256]{1,0:T(8,128)}) custom-call(s32[4]{0:T(128)S(1)} %add_convert_fusion.flags_ref, f32[258,8,256]{2,1,0:T(8,128)S(1)} %get-tuple-element.22.once_ref, f32[256,8,128]{2,1,0:T(8,128)S(1)} %get-tuple-element.23.inner_ref, f32[3,8,256]{2,1,0:T(8,128)S(1)} %collective-permute-done.up_ref, ...), custom_call_target="tpu_custom_call" | custom-call | tf_op jit(solution)/shard_map/second_pass/pallas_call | solution.py:569
  (4 shorter events, 0.0 us)
Async XLA Ops:
  6.7 11.0 %copy-start.4 = (f32[8,128]{1,0:T(8,128)S(1)}, f32[8,128]{1,0:T(8,128)}, u32[]{:S(2)}) copy-start(f32[8,128]{1,0:T(8,128)} %get-tuple-element.16.after_ref) | copy-start | bytes 12292
  6.7 55.4 %all-to-all-start = ((bf16[128,13,8,128]{3,2,1,0:T(8,128)(2,1)}), bf16[128,13,8,128]{3,2,1,0:T(8,128)(2,1)S(1)}, u32[]{:S(2)}, u32[]{:S(2)}) async-start(bf16[128,13,8,128]{3,2,1,0:T(8,128)(2,1)} %bitcast.10), calls=%async_computation | async-start | bytes 6815744 | tf_op jit(solution)/shard_map/all_to_all | solution.py:640
  17.7 1.0 %copy-start = (f32[256,256]{1,0:T(8,128)S(1)}, f32[256,256]{1,0:T(8,128)}, u32[]{:S(2)}) copy-start(f32[256,256]{1,0:T(8,128)} %cx_ref.5) | copy-start | bytes 786436
  18.7 0.9 %copy-start.2 = (f32[256,256]{1,0:T(8,128)S(1)}, f32[256,256]{1,0:T(8,128)}, u32[]{:S(2)}) copy-start(f32[256,256]{1,0:T(8,128)} %cy_ref.5) | copy-start | bytes 786436
  62.2 15.8 %copy-start.1 = (f32[256,256]{1,0:T(8,128)S(1)}, f32[256,256]{1,0:T(8,128)}, u32[]{:S(2)}) copy-start(f32[256,256]{1,0:T(8,128)} %cx_ref.5) | copy-start | bytes 786436
  62.2 15.8 %copy-start.3 = (f32[256,256]{1,0:T(8,128)S(1)}, f32[256,256]{1,0:T(8,128)}, u32[]{:S(2)}) copy-start(f32[256,256]{1,0:T(8,128)} %cy_ref.5) | copy-start | bytes 786436
  68.0 4.5 %collective-permute-start = (f32[3,8,256]{2,1,0:T(8,128)S(1)}, f32[3,8,256]{2,1,0:T(8,128)S(1)}, u32[]{:S(2)}, u32[]{:S(2)}) collective-permute-start(f32[3,8,256]{2,1,0:T(8,128)S(1)} %get-tuple-element.20), channel_id=1, source_target_pairs={{0,1},{1,2},{2,3},{3,4},{4,5},{5,6},{6,7},{7,0},{8,9},{9,10},{10,1... | collective-permute-start | bytes 73736 | tf_op jit(solution)/shard_map/ppermute | solution.py:651
  69.4 3.2 %collective-permute-start.1 = (f32[3,8,256]{2,1,0:T(8,128)S(1)}, f32[3,8,256]{2,1,0:T(8,128)S(1)}, u32[]{:S(2)}, u32[]{:S(2)}) collective-permute-start(f32[3,8,256]{2,1,0:T(8,128)S(1)} %get-tuple-element.21), channel_id=1, source_target_pairs={{0,7},{1,0},{2,1},{3,2},{4,3},{5,4},{6,5},{7,6},{8,15},{9,8},{10,9... | collective-permute-start | bytes 73736 | tf_op jit(solution)/shard_map/ppermute | solution.py:652
  72.5 8.0 %collective-permute-start.2 = (f32[7,8,128]{2,1,0:T(8,128)S(1)}, f32[7,8,128]{2,1,0:T(8,128)S(1)}, u32[]{:S(2)}, u32[]{:S(2)}) collective-permute-start(f32[7,8,128]{2,1,0:T(8,128)S(1)} %pad_maximum_fusion), channel_id=1, source_target_pairs={{0,8},{8,16},{16,24},{24,32},{32,40},{40,48},{48,56},{56,64},{64,7... | collective-permute-start | bytes 86024 | tf_op jit(solution)/shard_map/ppermute | solution.py:655
  73.3 7.2 %collective-permute-start.3 = (f32[7,8,128]{2,1,0:T(8,128)S(1)}, f32[7,8,128]{2,1,0:T(8,128)S(1)}, u32[]{:S(2)}, u32[]{:S(2)}) collective-permute-start(f32[7,8,128]{2,1,0:T(8,128)S(1)} %pad_maximum_fusion.1), channel_id=1, source_target_pairs={{0,120},{8,0},{16,8},{24,16},{32,24},{40,32},{48,40},{56,48},{64,5... | collective-permute-start | bytes 86024 | tf_op jit(solution)/shard_map/ppermute | solution.py:656

commit v7 on v6

--- a/solution.py
+++ b/solution.py
@@ -13,7 +13,7 @@
 CODES = 16
 ENTRIES = 896
 GROUP = 96
-FIRST_ROWS = 64
+FIRST_ROWS = 128
 ROWS = 32
 FLOOR = 0.15
 HALO = 2

time: 86.4 us -> 87.1 us (level)
    ppermute x1, starting transfers between devices: 1.33 us -> 0.02 us  [body(): up = lax.ppermute(bottom, 'gy', ring(along, 1))]
    ppermute x1, starting transfers between devices: 1.64 us -> 2.94 us  [body(): down = lax.ppermute(top, 'gy', ring(along, -1))]
    pallas_call x1, Pallas kernels: 5.87 us -> 6.89 us  [bin_blocks(): pl.pallas_call(bin_kernel, out_shape=(shape(height + 1, 32, 128), shape(H...]
    ppermute x1, starting transfers between devices: 4.65 us -> 3.78 us  [body(): east = lax.ppermute(near, 'gx', ring(across, -1))]
    ppermute x1, starting transfers between devices: 0.75 us -> 1.62 us  [body(): west = lax.ppermute(far, 'gx', ring(across, 1))]
where the time goes in v7:
time: 87.1 us; the launch traced here: 86.2 us
  waiting for transfers between devices  42.5 us (49%)
  Pallas kernels  20.3 us (23%)
  starting transfers between devices  20 us (23%)
  local copies, waits for them, and re-layouts  1.92 us (2%)
  between operations  1.38 us (2%)
    all_to_all x1, waiting for transfers between devices, body(): lax.all_to_all(message.reshape(devices, SLOTS, 8, 128), ('gx', 'gy'), spl...  41.8 us
    all_to_all x1, starting transfers between devices, body(): lax.all_to_all(message.reshape(devices, SLOTS, 8, 128), ('gx', 'gy'), spl...  11.6 us
    pallas_call x1, Pallas kernels, bin_blocks(): pl.pallas_call(bin_kernel, out_shape=(shape(height + 1, 32, 128), shape(H...  6.89 us
    pallas_call x1, Pallas kernels, pack(): pl.pallas_call(pack_kernel, out_shape=(jax.ShapeDtypeStruct((devices * SL...  4.96 us
    pallas_call x1, Pallas kernels, second_pass(): pl.pallas_call(second_kernel, out_shape=(jax.ShapeDtypeStruct((6, height,...  4.53 us
    ppermute x1, starting transfers between devices, body(): east = lax.ppermute(near, 'gx', ring(across, -1))  3.78 us
    ppermute x1, starting transfers between devices, body(): down = lax.ppermute(top, 'gy', ring(along, -1))  2.94 us
    pallas_call x1, Pallas kernels, first_pass(): pl.pallas_call(first_kernel, out_shape=(jax.ShapeDtypeStruct((height + 2,...  2.42 us
  transfers between devices with their start and end apart: 5, of which 2 were waited for; matrix products, arithmetic and copies ran while one was open for 0% of the time, Pallas kernels for 5%

profile of v7, /device:TPU:0, one launch (start us, length us, event | category | flops | bytes accessed | tf_op | source)
XLA Modules:
  0.0 86.2 jit_solution(1041723478559096988)
XLA Ops:
  1.3 5.0 %pack.1 = (bf16[1664,8,128]{2,1,0:T(8,128)(2,1)}, f32[8,128]{1,0:T(8,128)}) custom-call(s32[1]{0:T(128)S(6)} %copy.10.count_ref, s32[1,1024]{1,0:T(1,128)} %bitcast.12, s32[1,1024]{1,0:T(1,128)} %bitcast.13, bf16[6,1024,128]{2,1,0:T(8,128)(2,1)} %bitcast.11, bf16[1024,128]{1,0:T(8,128)(2,1)} %weight_ref.1, s32[1024,128]{1,0:T(8,128)} %cols_ref.1), custom_call_target="tpu_custom_call" | custom-call | tf_op jit(solution)/shard_map/pack/pallas_call | solution.py:135
  6.2 0.0 copy-start.4
  6.3 11.6 %all-to-all-start = ((bf16[128,13,8,128]{3,2,1,0:T(8,128)(2,1)}), bf16[128,13,8,128]{3,2,1,0:T(8,128)(2,1)S(1)}, u32[]{:S(2)}, u32[]{:S(2)}) async-start(bf16[128,13,8,128]{3,2,1,0:T(8,128)(2,1)} %bitcast.10), calls=%async_computation | async-start | bytes 6815744 | tf_op jit(solution)/shard_map/all_to_all | solution.py:640
  17.9 0.1 add_convert_fusion.flags_ref
  18.0 0.0 copy-done.4
  18.0 0.0 copy-start
  18.0 1.0 %copy-done = f32[256,256]{1,0:T(8,128)S(1)} copy-done((f32[256,256]{1,0:T(8,128)S(1)}, f32[256,256]{1,0:T(8,128)}, u32[]{:S(2)}) %copy-start) | copy-done | bytes 262168
  18.9 0.0 copy-start.2
  18.9 0.9 %copy-done.2 = f32[256,256]{1,0:T(8,128)S(1)} copy-done((f32[256,256]{1,0:T(8,128)S(1)}, f32[256,256]{1,0:T(8,128)}, u32[]{:S(2)}) %copy-start.2) | copy-done | bytes 262168
  19.9 0.7 coefficient_edges.1
  20.6 41.8 %all-to-all-done = bf16[128,13,8,128]{3,2,1,0:T(8,128)(2,1)S(1)} async-done(((bf16[128,13,8,128]{3,2,1,0:T(8,128)(2,1)}), bf16[128,13,8,128]{3,2,1,0:T(8,128)(2,1)S(1)}, u32[]{:S(2)}, u32[]{:S(2)}) %all-to-all-start) | async-done | bytes 3407904 | tf_op jit(solution)/shard_map/all_to_all | solution.py:640
  62.4 0.0 copy-start.1
  62.4 0.0 copy-start.3
  62.4 6.9 %bin.1 = (f32[257,32,128]{2,1,0:T(8,128)S(1)}, f32[3,8,256]{2,1,0:T(8,128)S(1)}, f32[3,8,256]{2,1,0:T(8,128)S(1)}) custom-call(bf16[1664,8,128]{2,1,0:T(8,128)(2,1)S(1)} %bitcast.9, f32[8,256]{1,0:T(8,128)S(1)} %get-tuple-element.17.edge_top, f32[8,256]{1,0:T(8,128)S(1)} %get-tuple-element.18.edge_bottom), custom_call_target="tpu_custom_call" | custom-call | tf_op jit(solution)/shard_map/bin/pallas_call | solution.py:291
  69.3 0.0 collective-permute-start
  69.4 2.9 %collective-permute-start.1 = (f32[3,8,256]{2,1,0:T(8,128)S(1)}, f32[3,8,256]{2,1,0:T(8,128)S(1)}, u32[]{:S(2)}, u32[]{:S(2)}) collective-permute-start(f32[3,8,256]{2,1,0:T(8,128)S(1)} %get-tuple-element.21), channel_id=1, source_target_pairs={{0,7},{1,0},{2,1},{3,2},{4,3},{5,4},{6,5},{7,6},{8,15},{9,8},{10,9... | collective-permute-start | bytes 73736 | tf_op jit(solution)/shard_map/ppermute | solution.py:652
  72.3 0.8 column_strips.1
  73.1 0.7 collective-permute-done.up_ref
  73.8 0.0 collective-permute-done.1.down_ref
  73.8 1.6 %collective-permute-start.2 = (f32[7,8,128]{2,1,0:T(8,128)S(1)}, f32[7,8,128]{2,1,0:T(8,128)S(1)}, u32[]{:S(2)}, u32[]{:S(2)}) collective-permute-start(f32[7,8,128]{2,1,0:T(8,128)S(1)} %pad_maximum_fusion), channel_id=1, source_target_pairs={{0,8},{8,16},{16,24},{24,32},{32,40},{40,48},{48,56},{56,64},{64,7... | collective-permute-start | bytes 86024 | tf_op jit(solution)/shard_map/ppermute | solution.py:655
  75.5 3.8 %collective-permute-start.3 = (f32[7,8,128]{2,1,0:T(8,128)S(1)}, f32[7,8,128]{2,1,0:T(8,128)S(1)}, u32[]{:S(2)}, u32[]{:S(2)}) collective-permute-start(f32[7,8,128]{2,1,0:T(8,128)S(1)} %pad_maximum_fusion.1), channel_id=1, source_target_pairs={{0,120},{8,0},{16,8},{24,16},{32,24},{40,32},{48,40},{56,48},{64,5... | collective-permute-start | bytes 86024 | tf_op jit(solution)/shard_map/ppermute | solution.py:656
  79.2 0.0 copy-done.1
  79.2 0.0 copy-done.3
  79.2 2.4 %first_pass.1 = (f32[258,8,256]{2,1,0:T(8,128)S(1)}, f32[256,8,128]{2,1,0:T(8,128)S(1)}) custom-call(s32[4]{0:T(128)S(1)} %add_convert_fusion.flags_ref, f32[257,32,128]{2,1,0:T(8,128)S(1)} %get-tuple-element.19.acc_ref, f32[3,8,256]{2,1,0:T(8,128)S(1)} %collective-permute-done.up_ref, f32[3,8,256]{2,1,0:T(8,128)S(1)} %collective-permute-done.1.down_ref, ...), custom_call_target="tpu_custom_call" | custom-call | tf_op jit(solution)/shard_map/first_pass/pallas_call | solution.py:426
  81.7 0.0 collective-permute-done.2.west_ref
  81.7 0.0 collective-permute-done.3.east_ref
  81.7 4.5 %second_pass.1 = (f32[6,256,256]{2,1,0:T(8,128)}, f32[256,256]{1,0:T(8,128)}) custom-call(s32[4]{0:T(128)S(1)} %add_convert_fusion.flags_ref, f32[258,8,256]{2,1,0:T(8,128)S(1)} %get-tuple-element.22.once_ref, f32[256,8,128]{2,1,0:T(8,128)S(1)} %get-tuple-element.23.inner_ref, f32[3,8,256]{2,1,0:T(8,128)S(1)} %collective-permute-done.up_ref, ...), custom_call_target="tpu_custom_call" | custom-call | tf_op jit(solution)/shard_map/second_pass/pallas_call | solution.py:569
  (4 shorter events, 0.0 us)
Async XLA Ops:
  6.2 11.7 %copy-start.4 = (f32[8,128]{1,0:T(8,128)S(1)}, f32[8,128]{1,0:T(8,128)}, u32[]{:S(2)}) copy-start(f32[8,128]{1,0:T(8,128)} %get-tuple-element.16.after_ref) | copy-start | bytes 12292
  6.3 56.2 %all-to-all-start = ((bf16[128,13,8,128]{3,2,1,0:T(8,128)(2,1)}), bf16[128,13,8,128]{3,2,1,0:T(8,128)(2,1)S(1)}, u32[]{:S(2)}, u32[]{:S(2)}) async-start(bf16[128,13,8,128]{3,2,1,0:T(8,128)(2,1)} %bitcast.10), calls=%async_computation | async-start | bytes 6815744 | tf_op jit(solution)/shard_map/all_to_all | solution.py:640
  18.0 1.0 %copy-start = (f32[256,256]{1,0:T(8,128)S(1)}, f32[256,256]{1,0:T(8,128)}, u32[]{:S(2)}) copy-start(f32[256,256]{1,0:T(8,128)} %cx_ref.5) | copy-start | bytes 786436
  18.9 0.9 %copy-start.2 = (f32[256,256]{1,0:T(8,128)S(1)}, f32[256,256]{1,0:T(8,128)}, u32[]{:S(2)}) copy-start(f32[256,256]{1,0:T(8,128)} %cy_ref.5) | copy-start | bytes 786436
  62.4 16.8 %copy-start.1 = (f32[256,256]{1,0:T(8,128)S(1)}, f32[256,256]{1,0:T(8,128)}, u32[]{:S(2)}) copy-start(f32[256,256]{1,0:T(8,128)} %cx_ref.5) | copy-start | bytes 786436
  62.4 16.8 %copy-start.3 = (f32[256,256]{1,0:T(8,128)S(1)}, f32[256,256]{1,0:T(8,128)}, u32[]{:S(2)}) copy-start(f32[256,256]{1,0:T(8,128)} %cy_ref.5) | copy-start | bytes 786436
  69.3 4.5 %collective-permute-start = (f32[3,8,256]{2,1,0:T(8,128)S(1)}, f32[3,8,256]{2,1,0:T(8,128)S(1)}, u32[]{:S(2)}, u32[]{:S(2)}) collective-permute-start(f32[3,8,256]{2,1,0:T(8,128)S(1)} %get-tuple-element.20), channel_id=1, source_target_pairs={{0,1},{1,2},{2,3},{3,4},{4,5},{5,6},{6,7},{7,0},{8,9},{9,10},{10,1... | collective-permute-start | bytes 73736 | tf_op jit(solution)/shard_map/ppermute | solution.py:651
  69.4 4.5 %collective-permute-start.1 = (f32[3,8,256]{2,1,0:T(8,128)S(1)}, f32[3,8,256]{2,1,0:T(8,128)S(1)}, u32[]{:S(2)}, u32[]{:S(2)}) collective-permute-start(f32[3,8,256]{2,1,0:T(8,128)S(1)} %get-tuple-element.21), channel_id=1, source_target_pairs={{0,7},{1,0},{2,1},{3,2},{4,3},{5,4},{6,5},{7,6},{8,15},{9,8},{10,9... | collective-permute-start | bytes 73736 | tf_op jit(solution)/shard_map/ppermute | solution.py:652
  73.8 7.8 %collective-permute-start.2 = (f32[7,8,128]{2,1,0:T(8,128)S(1)}, f32[7,8,128]{2,1,0:T(8,128)S(1)}, u32[]{:S(2)}, u32[]{:S(2)}) collective-permute-start(f32[7,8,128]{2,1,0:T(8,128)S(1)} %pad_maximum_fusion), channel_id=1, source_target_pairs={{0,8},{8,16},{16,24},{24,32},{32,40},{40,48},{48,56},{56,64},{64,7... | collective-permute-start | bytes 86024 | tf_op jit(solution)/shard_map/ppermute | solution.py:655
  75.5 6.2 %collective-permute-start.3 = (f32[7,8,128]{2,1,0:T(8,128)S(1)}, f32[7,8,128]{2,1,0:T(8,128)S(1)}, u32[]{:S(2)}, u32[]{:S(2)}) collective-permute-start(f32[7,8,128]{2,1,0:T(8,128)S(1)} %pad_maximum_fusion.1), channel_id=1, source_target_pairs={{0,120},{8,0},{16,8},{24,16},{32,24},{40,32},{48,40},{56,48},{64,5... | collective-permute-start | bytes 86024 | tf_op jit(solution)/shard_map/ppermute | solution.py:656
